TPU v7x, 512 devices: a whole 4x8x8 slice. The times are simulated.
512 devices in a mesh: space: 32 (over z, x), brow: 8 (over y), bcol: 2 (over core).
Axes of the slice: x: 4, y: 8, z: 8, core: 2. Of those that a mesh axis runs over, the one named last changes fastest.
Arguments:
- orbitals: float32 [589824, 256], P(('space', 'brow'), 'bcol'), may hold values from -0.0078125 to 0.0078125
- applied: float32 [589824, 256], P(('space', 'brow'), 'bcol'), may hold values from -0.0078125 to 0.0078125
- cotangent: float32 [589824, 256], P(('space', 'brow'), 'bcol'), may hold values from -6 to 6
- rotation: float32 [256, 256], P('brow', 'bcol'), may hold values from -0.5 to 1.5, as said below
- levels: float32 [256], replicated, may hold values from -3 to 9.8, as said below
Outputs:
- orbital_grad: float32 [589824, 256], P(('space', 'brow'), 'bcol')
Inputs may be any that keep to these rules, and one draw needn't show every extreme that they name: rotation has a unit diagonal plus independent entries of deviation 0.4 / sqrt(256). levels rise with the index, neighbours at least 0.025 apart.
All inputs are finite; a program needn't handle non-finite values.
Results may differ from a plain program's by a relative error of at most 0.0003.
Values sent between devices are 32-bit elements; how exact they have to be, the bound alone decides.
No kernel may reach another device: no remote copies, remote signals or barrier semaphores. Data moves between devices by JAX's collectives and lax.ppermute only.
A program may use at most 64 MiB of HBM per device.

v0:
```python
import jax
import jax.numpy as jnp
from jax import lax
from jax.sharding import PartitionSpec as P


def matmul(left, right):
    return jnp.dot(left, right, preferred_element_type=jnp.float32, precision=lax.Precision.HIGHEST)


def inner_cells(left, right):
    return lax.dot_general(
        left,
        right,
        (((0,), (0,)), ((), ())),
        preferred_element_type=jnp.float32,
        precision=lax.Precision.HIGHEST,
    )


def outer_bands(left, right):
    return lax.dot_general(
        left,
        right,
        (((1,), (1,)), ((), ())),
        preferred_element_type=jnp.float32,
        precision=lax.Precision.HIGHEST,
    )


def subspace(rotation, levels, grad_rot):
    gram_rot = inner_cells(rotation, grad_rot)
    level_gaps = levels[None, :] - levels[:, None]
    diag_mask = jnp.eye(levels.shape[0], dtype=bool)
    inverse = jnp.where(
        diag_mask, jnp.float32(0.0), 1.0 / jnp.where(diag_mask, jnp.float32(1.0), level_gaps)
    )
    mixing = inverse * gram_rot
    sym_ham = mixing + mixing.T
    sym_ovl = mixing * levels[None, :] + levels[:, None] * mixing.T + jnp.diag(jnp.diag(gram_rot))
    ham_coef = outer_bands(matmul(rotation, sym_ham), rotation)
    ovl_coef = -outer_bands(matmul(rotation, sym_ovl), rotation)
    return (ham_coef, ovl_coef)


def band_plan(orbitals, applied, cotangent, row_panel, levels):
    band_width = orbitals.shape[1]
    band_first = lax.axis_index("bcol") * band_width
    orb_whole = lax.all_gather(orbitals, "bcol", axis=1, tiled=True)
    col_sums = lax.psum(inner_cells(orb_whole, cotangent), ("space", "brow"))
    grad_rot, full_rot = (
        lax.all_gather(col_sums, "bcol", axis=1, tiled=True),
        lax.all_gather(row_panel, "bcol", axis=1, tiled=True),
    )
    ham_coef, ovl_coef = subspace(full_rot, levels, grad_rot)
    app_whole, cot_whole = (
        lax.all_gather(applied, "bcol", axis=1, tiled=True),
        lax.all_gather(cotangent, "bcol", axis=1, tiled=True),
    )
    ovl_cols = lax.dynamic_slice_in_dim(ovl_coef, band_first, band_width, 1)
    ham_cols = lax.dynamic_slice_in_dim(ham_coef, band_first, band_width, 1)
    rot_rows = lax.dynamic_slice_in_dim(full_rot, band_first, band_width, 0)
    result = (
        matmul(orb_whole, ovl_cols) + matmul(app_whole, ham_cols) + outer_bands(cot_whole, rot_rows)
    )
    return result


def body(orbitals, applied, cotangent, rotation, levels):
    row_panel = lax.all_gather(rotation, "brow", axis=0, tiled=True)
    result = band_plan(orbitals, applied, cotangent, row_panel, levels)
    return result


def solution(mesh):
    return jax.shard_map(
        body,
        mesh=mesh,
        in_specs=(
            P(("space", "brow"), "bcol"),
            P(("space", "brow"), "bcol"),
            P(("space", "brow"), "bcol"),
            P("brow", "bcol"),
            P(),
        ),
        out_specs=P(("space", "brow"), "bcol"),
        check_vma=False,
    )
```

profile of v0, /device:TPU:1, one launch (start us, length us, event | category | flops | bytes accessed | tf_op | source)
XLA Modules:
  0.0 323.9 jit_solution(460007272820262635)
XLA Ops:
  6.5 0.0 copy-start.1
  6.5 0.0 all-gather.4.cloned.1.call-start
  6.5 0.7 all-gather.4.cloned.1.call-update
  7.3 0.0 all-reduce.2.cloned.1.call-start
  7.3 27.9 %all-gather.4.cloned.1.call-done = f32[2304,256]{1,0:T(8,128)} async-done(((f32[2304,128]{1,0:T(8,128)}), f32[2304,256]{1,0:T(8,128)}) %all-gather.4.cloned.1.call-update) | async-done | bytes 2359312 | tf_op jit(solution)/shard_map/all_gather | solution.py:49
  35.2 0.0 copy-done.1
  35.2 6.1 %fusion.20 = f32[256,128]{1,0:T(8,128)} fusion(f32[2304,256]{1,0:T(8,128)} %all-gather.4.cloned.1.call-done, f32[2304,128]{1,0:T(8,128)S(1)} %copy-done.1), kind=kOutput, calls=%fused_computation.29 | convolution fusion | flops 905969664 | bytes 3670016 | tf_op jit(solution)/shard_map/dot_general | solution.py:12
  41.4 0.0 all-reduce.2.cloned.1.call-update
  41.4 0.0 copy-start.2
  41.4 0.0 all-gather.6.cloned.1.call-start
  41.4 0.7 all-gather.6.cloned.1.call-update
  42.1 0.0 all-gather.8.cloned.1.call-start
  42.2 0.5 all-gather.8.cloned.1.call-update
  42.7 0.0 copy-done.2
  42.7 18.6 %all_gather.20 = f32[256,128]{1,0:T(8,128)S(1)} all-gather(f32[32,128]{1,0:T(8,128)S(1)} %copy-done.2), channel_id=1, replica_groups=mesh['space'=32,'brow'=8,'bcol'=2] {'brow'}, dimensions={0}, use_global_device_ids=true | all-gather | bytes 147456 | tf_op jit(solution)/shard_map/all_gather | solution.py:70
  61.4 7.9 %all_gather.21 = f32[256,256]{1,0:T(8,128)S(1)} all-gather(f32[256,128]{1,0:T(8,128)S(1)} %all_gather.20), channel_id=1, replica_groups=mesh['space'=32,'brow'=8,'bcol'=2] {'bcol'}, dimensions={1}, use_global_device_ids=true | all-gather | bytes 393216 | tf_op jit(solution)/shard_map/all_gather | solution.py:53
  69.2 197.0 %all-reduce.2.cloned.1.call-done = f32[256,128]{1,0:T(8,128)} async-done(((f32[256,128]{1,0:T(8,128)}), f32[256,128]{1,0:T(8,128)}) %all-reduce.2.cloned.1.call-update) | async-done | bytes 131088 | tf_op jit(solution)/shard_map/psum | solution.py:50
  266.3 7.2 %all_gather.19 = f32[256,256]{1,0:T(8,128)S(1)} all-gather(f32[256,128]{1,0:T(8,128)} %all-reduce.2.cloned.1.call-done), channel_id=1, replica_groups=mesh['space'=32,'brow'=8,'bcol'=2] {'bcol'}, dimensions={1}, use_global_device_ids=true | all-gather | bytes 393216 | tf_op jit(solution)/shard_map/all_gather | solution.py:52
  273.5 0.0 copy-start.3
  273.5 0.6 fusion.21
  274.1 0.1 copy.8
  274.2 2.3 gather_fusion
  276.6 0.0 copy-done.3
  276.6 0.7 fusion.3
  277.3 0.6 fusion.22
  277.9 0.0 copy-start
  277.9 0.7 fusion.1
  278.6 0.6 fusion.23
  279.2 0.3 copy-done
  279.6 2.6 fusion.9
  282.2 7.3 %all-gather.6.cloned.1.call-done = f32[2304,256]{1,0:T(8,128)} async-done(((f32[2304,128]{1,0:T(8,128)}), f32[2304,256]{1,0:T(8,128)}) %all-gather.6.cloned.1.call-update) | async-done | bytes 2359312 | tf_op jit(solution)/shard_map/all_gather | solution.py:57
  289.5 4.3 %convolution_add_fusion.1 = f32[128,2304]{1,0:T(8,128)S(1)} fusion(f32[128,2304]{1,0:T(8,128)S(1)} %fusion.9, f32[2304,256]{1,0:T(8,128)} %all-gather.6.cloned.1.call-done, f32[256,256]{1,0:T(8,128)S(1)} %fusion.23, s32[]{:T(128)S(6)} %select_n.34), kind=kOutput, calls=%fused_computation.2 | convolution fusion | flops 906264576 | bytes 4849668 | tf_op jit(solution)/shard_map/dot_general | solution.py:8
  293.8 18.0 %all-gather.8.cloned.1.call-done = f32[2304,256]{1,0:T(8,128)} async-done(((f32[2304,128]{1,0:T(8,128)}), f32[2304,256]{1,0:T(8,128)}) %all-gather.8.cloned.1.call-update) | async-done | bytes 2359312 | tf_op jit(solution)/shard_map/all_gather | solution.py:58
  311.8 4.2 %fusion = f32[2304,128]{0,1:T(8,128)S(1)} fusion(f32[128,2304]{1,0:T(8,128)S(1)} %convolution_add_fusion.1, f32[2304,256]{1,0:T(8,128)} %all-gather.8.cloned.1.call-done, f32[256,256]{1,0:T(8,128)S(1)} %all_gather.21, s32[]{:T(128)S(6)} %select_n.34), kind=kOutput, calls=%fused_computation.3 | convolution fusion | flops 906264576 | bytes 4849668 | tf_op jit(solution)/shard_map/dot_general | solution.py:22
  316.0 1.4 copy.9
  (1 shorter events, 0.0 us)
Async XLA Ops:
  6.5 28.7 %copy-start.1 = (f32[2304,128]{1,0:T(8,128)S(1)}, f32[2304,128]{1,0:T(8,128)}, u32[]{:S(2)}) copy-start(f32[2304,128]{1,0:T(8,128)} %param.7) | copy-start | bytes 3538948
  6.5 28.7 %all-gather.4.cloned.1.call-start = ((), (), s32[]{:S(2)}) async-start(), calls=%async_computation | async-start | bytes 3538944 | tf_op jit(solution)/shard_map/all_gather | solution.py:49
  7.3 259.0 %all-reduce.2.cloned.1.call-start = ((), (), s32[]{:S(2)}) async-start(), calls=%async_computation.1 | async-start | bytes 262144 | tf_op jit(solution)/shard_map/psum | solution.py:50
  41.4 1.3 copy-start.2
  41.4 248.1 %all-gather.6.cloned.1.call-start = ((), (), s32[]{:S(2)}) async-start(), calls=%async_computation.2 | async-start | bytes 3538944 | tf_op jit(solution)/shard_map/all_gather | solution.py:57
  42.1 269.6 %all-gather.8.cloned.1.call-start = ((), (), s32[]{:S(2)}) async-start(), calls=%async_computation.3 | async-start | bytes 3538944 | tf_op jit(solution)/shard_map/all_gather | solution.py:58
  273.5 3.1 copy-start.3
  277.9 1.7 copy-start
Sparse Core Ops, SparseCore 0:
  9.4 25.7 all-gather.3
  41.5 224.7 all-reduce.1
  268.5 20.8 all-gather.5
  291.6 20.1 all-gather.7
where the time goes:
time: 324 us
  waiting for transfers between devices  252 us (78%)
  blocking collectives  33.7 us (10%)
  matrix products  20.4 us (6%)
  between operations  13.2 us (4%)
  local copies, waits for them, and re-layouts  4.21 us (1%)
    psum x1, waiting for transfers between devices, band_plan(): col_sums = lax.psum(inner_cells(orb_whole, cotangent), ('space', 'brow'))  197 us
    all_gather x1, waiting for transfers between devices, band_plan(): orb_whole = lax.all_gather(orbitals, 'bcol', axis=1, tiled=True)  27.9 us
    all_gather x1, blocking collectives, body(): row_panel = lax.all_gather(rotation, 'brow', axis=0, tiled=True)  18.6 us
    all_gather x1, waiting for transfers between devices, band_plan(): lax.all_gather(cotangent, 'bcol', axis=1, tiled=True)  18 us
    dot_general x4, matrix products, matmul(): jnp.dot(left, right, preferred_element_type=jnp.float32, precision=lax.Pr...  8.33 us
    all_gather x1, blocking collectives, band_plan(): lax.all_gather(row_panel, 'bcol', axis=1, tiled=True)  7.88 us
    all_gather x1, waiting for transfers between devices, band_plan(): lax.all_gather(applied, 'bcol', axis=1, tiled=True)  7.28 us
    all_gather x1, blocking collectives, band_plan(): lax.all_gather(col_sums, 'bcol', axis=1, tiled=True)  7.22 us
  transfers between devices with their start and end apart: 4, of which 4 were waited for; matrix products, arithmetic and copies ran while one was open for 4% of the time, Pallas kernels for 0%

commit v1 on v0

v1 whole, which is shorter than its diff:
```python
import functools

import jax
import jax.numpy as jnp
from jax import lax
from jax.experimental import pallas as pl
from jax.experimental.pallas import tpu as pltpu
from jax.sharding import PartitionSpec as P

F32 = jnp.float32
BF16 = jnp.bfloat16
VMEM = pl.BlockSpec(memory_space=pltpu.VMEM)
ANY = pl.BlockSpec(memory_space=pl.ANY)
CHUNK = 576


def halves(x):
    high = x.astype(BF16)
    return high, (x - high.astype(F32)).astype(BF16)


def dot(left, right, dims, precision=None):
    return lax.dot_general(
        left, right, (dims, ((), ())), preferred_element_type=F32, precision=precision
    )


def exact(left, right, dims=((1,), (0,))):
    return dot(left, right, dims, lax.Precision.HIGHEST)


def gram_kernel(bcol_ref, own_hbm, oth_hbm, cot_hbm, out_ref, own, oth, cot, sems):
    cells, width = own.shape
    steps = cells // CHUNK
    copies = []
    for step in range(steps):
        rows = pl.ds(step * CHUNK, CHUNK)
        group = [
            pltpu.make_async_copy(src.at[rows], dst.at[rows], sems.at[step, at])
            for at, (src, dst) in enumerate(((own_hbm, own), (oth_hbm, oth), (cot_hbm, cot)))
        ]
        for copy in group:
            copy.start()
        copies.append(group)
    total = None
    for step in range(steps):
        rows = pl.ds(step * CHUNK, CHUNK)
        for copy in copies[step]:
            copy.wait()
        cot_high, cot_low = halves(cot[rows, :])
        own_high, own_low = halves(own[rows, :])
        oth_high, oth_low = halves(oth[rows, :])
        high = jnp.concatenate([own_high, oth_high], axis=1)
        low = jnp.concatenate([own_low, oth_low], axis=1)
        cells_first = ((0,), (0,))
        part = (
            dot(cot_high, high, cells_first)
            + dot(cot_low, high, cells_first)
            + dot(cot_high, low, cells_first)
        )
        total = part if total is None else total + part
    mine = bcol_ref[0]
    out_ref[pl.ds(pl.multiple_of(mine * width, width), width), :] = total[:, :width]
    out_ref[pl.ds(pl.multiple_of((1 - mine) * width, width), width), :] = total[:, width:]


def spread_kernel(parts_ref, panel_ref, out_ref):
    tile = jnp.sum(parts_ref[...], axis=0)
    both = jnp.concatenate([tile, panel_ref[...]], axis=0)
    out_ref[...] = jnp.broadcast_to(both[None], out_ref.shape)


def gather_kernel(parts_ref, out_ref):
    tiles = jnp.sum(parts_ref[:, :, :8, :], axis=0)
    both = tiles.reshape(16, tiles.shape[-1])
    out_ref[...] = jnp.broadcast_to(both[None], out_ref.shape)


def tail_kernel(
    bcol_ref,
    sums_ref,
    panels_ref,
    row_ref,
    col_ref,
    orb_own,
    orb_oth,
    app_own,
    app_oth,
    cot_own,
    cot_oth,
    out_hbm,
    held,
    result,
    weights,
    rotation_ref,
    in_sems,
    out_sems,
):
    sources = (orb_own, orb_oth, app_own, app_oth, cot_own, cot_oth)
    cells, width = result.shape
    steps = cells // CHUNK
    copies = []
    for step in range(steps):
        rows = pl.ds(step * CHUNK, CHUNK)
        group = [
            pltpu.make_async_copy(src.at[rows], held.at[at, rows], in_sems.at[step, at])
            for at, src in enumerate(sources)
        ]
        for copy in group:
            copy.start()
        copies.append(group)

    mine = bcol_ref[0]
    bands = 2 * width
    tiles = width // 8
    grad_t = jnp.concatenate(
        [
            jnp.concatenate(
                [
                    sums_ref[b * tiles : (b + 1) * tiles, c * 8 : (c + 1) * 8, :].reshape(width, width)
                    for b in range(2)
                ],
                axis=1,
            )
            for c in range(2)
        ],
        axis=0,
    )
    rotation = jnp.concatenate(
        [panels_ref[:, c, 8:, :].reshape(bands, width) for c in range(2)], axis=1
    )
    rotation_ref[...] = rotation
    gram_t = exact(grad_t, rotation)
    levels_row = row_ref[...]
    levels_col = col_ref[...]
    at_row = lax.broadcasted_iota(jnp.int32, (bands, bands), 0)
    at_col = lax.broadcasted_iota(jnp.int32, (bands, bands), 1)
    diagonal = at_row == at_col
    gaps = jnp.where(diagonal, 1.0, levels_col - levels_row)
    mixing_t = jnp.where(diagonal, 0.0, (1.0 / gaps) * gram_t)
    sym_ham = mixing_t + mixing_t.T
    scaled = levels_col * mixing_t
    sym_ovl = scaled + scaled.T + jnp.where(diagonal, gram_t, 0.0)
    rot_rows = rotation_ref[pl.ds(pl.multiple_of(mine * width, width), width), :]
    right = exact(jnp.concatenate([sym_ovl, sym_ham], axis=0), rot_rows, ((1,), (1,)))
    coefs = exact(rotation, jnp.concatenate([-right[:bands], right[bands:]], axis=1))
    rot_t = rot_rows.T
    for at, block in enumerate((coefs[:, :width], coefs[:, width:], rot_t)):
        high, low = halves(block)
        both = jnp.concatenate([high, low], axis=1)
        weights[at] = both

    first = pl.ds(pl.multiple_of(mine * width, width), width)
    second = pl.ds(pl.multiple_of((1 - mine) * width, width), width)
    weight = jnp.concatenate(
        [weights[at, rows, :] for at in range(3) for rows in (first, second)], axis=0
    )
    outs = []
    for step in range(steps):
        rows = pl.ds(step * CHUNK, CHUNK)
        for copy in copies[step]:
            copy.wait()
        left = jnp.concatenate([held[at, rows, :] for at in range(6)], axis=1)
        high, low = halves(left)
        inner = ((1,), (0,))
        wide = dot(high, weight, inner)
        result[rows, :] = wide[:, :width] + wide[:, width:] + dot(low, weight[:, :width], inner)
        copy = pltpu.make_async_copy(result.at[rows], out_hbm.at[rows], out_sems.at[step])
        copy.start()
        outs.append(copy)
    for copy in outs:
        copy.wait()


def body(orbitals, applied, cotangent, panel, levels):
    cells, width = orbitals.shape
    bands = 2 * width
    steps = cells // CHUNK
    swap = [(0, 1), (1, 0)]
    orb_oth = lax.ppermute(orbitals, "bcol", swap)
    app_oth = lax.ppermute(applied, "bcol", swap)
    cot_oth = lax.ppermute(cotangent, "bcol", swap)
    mine = lax.axis_index("bcol").reshape(1)
    smem = pl.BlockSpec(memory_space=pltpu.SMEM)
    space = lax.axis_size("space")
    brow = lax.axis_size("brow")
    tile = bands // space

    partial = pl.pallas_call(
        gram_kernel,
        out_shape=jax.ShapeDtypeStruct((bands, width), F32),
        in_specs=[smem, ANY, ANY, ANY],
        out_specs=VMEM,
        scratch_shapes=[pltpu.VMEM((cells, width), F32)] * 3 + [pltpu.SemaphoreType.DMA((steps, 3))],
        compiler_params=pltpu.CompilerParams(vmem_limit_bytes=24 * 2**20),
        name="gram",
    )(mine, orbitals, orb_oth, cotangent)

    parts = lax.all_to_all(partial.reshape(space, tile, width), "space", 0, 0, tiled=True)
    rows = tile + panel.shape[0]
    spread = pl.pallas_call(
        spread_kernel,
        out_shape=jax.ShapeDtypeStruct((2 * brow, rows, width), F32),
        in_specs=[VMEM, VMEM],
        out_specs=VMEM,
        name="spread",
    )(parts, panel)
    panels = lax.all_to_all(spread, ("brow", "bcol"), 0, 0, tiled=True)
    panels = panels.reshape(brow, 2, rows, width)
    gather = pl.pallas_call(
        gather_kernel,
        out_shape=jax.ShapeDtypeStruct((space, 2 * tile, width), F32),
        in_specs=[VMEM],
        out_specs=VMEM,
        name="gather",
    )(panels)
    sums = lax.all_to_all(gather, "space", 0, 0, tiled=True)

    return pl.pallas_call(
        tail_kernel,
        out_shape=jax.ShapeDtypeStruct((cells, width), F32),
        in_specs=[smem] + [VMEM] * 4 + [ANY] * 6,
        out_specs=ANY,
        scratch_shapes=[
            pltpu.VMEM((6, cells, width), F32),
            pltpu.VMEM((cells, width), F32),
            pltpu.VMEM((3, bands, bands), BF16),
            pltpu.VMEM((bands, bands), F32),
            pltpu.SemaphoreType.DMA((steps, 6)),
            pltpu.SemaphoreType.DMA((steps,)),
        ],
        compiler_params=pltpu.CompilerParams(vmem_limit_bytes=40 * 2**20),
        name="tail",
    )(
        mine,
        sums,
        panels,
        levels.reshape(1, bands),
        levels.reshape(bands, 1),
        orbitals,
        orb_oth,
        applied,
        app_oth,
        cotangent,
        cot_oth,
    )


def solution(mesh):
    return jax.shard_map(
        body,
        mesh=mesh,
        in_specs=(
            P(("space", "brow"), "bcol"),
            P(("space", "brow"), "bcol"),
            P(("space", "brow"), "bcol"),
            P("brow", "bcol"),
            P(),
        ),
        out_specs=P(("space", "brow"), "bcol"),
        check_vma=False,
    )
```

time: 324 us -> 88.6 us (0.27)
  waiting for transfers between devices: 252 us -> 19.2 us
  starting transfers between devices: 0.12 us -> 25.6 us
  matrix products: 20.4 us -> 0 us
  Pallas kernels: 0 us -> 14.1 us
  between operations: 13.2 us -> 0.1 us
  blocking collectives: 33.7 us -> 22.4 us
    psum x1 -> x0, waiting for transfers between devices: 197 us -> none  [band_plan(): col_sums = lax.psum(inner_cells(orb_whole, cotangent), ('space', 'brow'))]
    all_gather x3 -> x0, waiting for transfers between devices: 53.2 us -> none  [the longest x1 27.9 us: band_plan(): orb_whole = lax.all_gather(orbitals, 'bcol', axis=1, tiled=True)]
    all_gather x3 -> x0, blocking collectives: 33.7 us -> none  [the longest x1 18.6 us: body(): row_panel = lax.all_gather(rotation, 'brow', axis=0, tiled=True)]
    all_to_all x0 -> x1, blocking collectives: none -> 22.4 us  [body(): panels = lax.all_to_all(spread, ('brow', 'bcol'), 0, 0, tiled=True)]
    dot_general x9 -> x0, matrix products: 20.4 us -> none  [the longest x4 8.33 us: matmul(): jnp.dot(left, right, preferred_element_type=jnp.float32, precision=lax.Pr...]
    all_to_all x0 -> x2, waiting for transfers between devices: none -> 16.6 us  [the longest x1 11.9 us: body(): sums = lax.all_to_all(gather, 'space', 0, 0, tiled=True)]
    pallas_call x0 -> x4, Pallas kernels: none -> 14.1 us  [the longest x1 7.57 us: body(): pl.pallas_call(tail_kernel, out_shape=jax.ShapeDtypeStruct((cells, width)...]
    ppermute x0 -> x3, starting transfers between devices: none -> 13.4 us  [the longest x1 8.78 us: body(): orb_oth = lax.ppermute(orbitals, 'bcol', swap)]
  transfers between devices with their start and end apart: 4 -> 5, of which waited for: 4 -> 3; matrix products, arithmetic and copies ran while one was open for 4% -> 1% of each run, Pallas kernels for 0% -> 4%
where the time goes in v1:
time: 88.6 us; the launch traced here: 87.9 us
  starting transfers between devices  25.6 us (29%)
  blocking collectives  22.4 us (25%)
  waiting for transfers between devices  19.2 us (22%)
  Pallas kernels  14.1 us (16%)
  local copies, waits for them, and re-layouts  6.5 us (7%)
    all_to_all x1, blocking collectives, body(): panels = lax.all_to_all(spread, ('brow', 'bcol'), 0, 0, tiled=True)  22.4 us
    all_to_all x1, waiting for transfers between devices, body(): sums = lax.all_to_all(gather, 'space', 0, 0, tiled=True)  11.9 us
    ppermute x1, starting transfers between devices, body(): orb_oth = lax.ppermute(orbitals, 'bcol', swap)  8.78 us
    all_to_all x1, starting transfers between devices, body(): lax.all_to_all(partial.reshape(space, tile, width), 'space', 0, 0, tiled=...  7.65 us
    pallas_call x1, Pallas kernels, body(): pl.pallas_call(tail_kernel, out_shape=jax.ShapeDtypeStruct((cells, width)...  7.57 us
    unnamed x16, local copies, waits for them, and re-layouts  5.7 us
    all_to_all x1, waiting for transfers between devices, body(): lax.all_to_all(partial.reshape(space, tile, width), 'space', 0, 0, tiled=...  4.65 us
    all_to_all x1, starting transfers between devices, body(): sums = lax.all_to_all(gather, 'space', 0, 0, tiled=True)  4.6 us
  transfers between devices with their start and end apart: 5, of which 3 were waited for; matrix products, arithmetic and copies ran while one was open for 1% of the time, Pallas kernels for 4%

profile of v1, /device:TPU:1, one launch (start us, length us, event | category | flops | bytes accessed | tf_op | source)
XLA Modules:
  0.0 87.9 jit_solution(455968049485313124)
XLA Ops:
  0.0 8.8 %collective-permute-start = (f32[2304,128]{1,0:T(8,128)}, f32[2304,128]{1,0:T(8,128)S(1)}, u32[]{:S(2)}, u32[]{:S(2)}) collective-permute-start(f32[2304,128]{1,0:T(8,128)} %orb_own.1), channel_id=1, source_target_pairs={{0,1},{1,0},{2,3},{3,2},{4,5},{5,4},{6,7},{7,6},{8,9},{9,8},{10,11... | collective-permute-start | bytes 3538952 | tf_op jit(solution)/shard_map/ppermute | solution.py:180
  8.8 2.7 %collective-permute-done.oth_hbm.orb_oth = f32[2304,128]{1,0:T(8,128)S(1)} collective-permute-done((f32[2304,128]{1,0:T(8,128)}, f32[2304,128]{1,0:T(8,128)S(1)}, u32[]{:S(2)}, u32[]{:S(2)}) %collective-permute-start) | collective-permute-done | bytes 1179680 | tf_op jit(solution)/shard_map/ppermute | solution.py:180
  11.4 0.0 copy-start
  11.5 1.3 %copy-done = f32[2304,128]{1,0:T(8,128)S(1)} copy-done((f32[2304,128]{1,0:T(8,128)S(1)}, f32[2304,128]{1,0:T(8,128)}, u32[]{:S(2)}) %copy-start) | copy-done | bytes 1179672
  12.7 0.0 copy-start.2
  12.7 1.3 %copy-done.2 = f32[2304,128]{1,0:T(8,128)S(1)} copy-done((f32[2304,128]{1,0:T(8,128)S(1)}, f32[2304,128]{1,0:T(8,128)}, u32[]{:S(2)}) %copy-start.2) | copy-done | bytes 1179672
  14.0 0.0 copy-start.3
  14.0 3.1 %gram.1 = f32[256,128]{1,0:T(8,128)} custom-call(s32[1]{0:T(128)} %bitcast.bcol_ref, f32[2304,128]{1,0:T(8,128)S(1)} %copy-done, f32[2304,128]{1,0:T(8,128)S(1)} %collective-permute-done.oth_hbm.orb_oth, f32[2304,128]{1,0:T(8,128)S(1)} %copy-done.2), custom_call_target="tpu_custom_call" | custom-call | tf_op jit(solution)/shard_map/gram/pallas_call | solution.py:189
  17.1 7.7 %all-to-all-start = ((f32[32,8,128]{2,1,0:T(8,128)}), f32[32,8,128]{2,1,0:T(8,128)}, u32[]{:S(2)}, u32[]{:S(2)}) async-start(f32[32,8,128]{2,1,0:T(8,128)} %bitcast.1), calls=%async_computation | async-start | bytes 262144 | tf_op jit(solution)/shard_map/all_to_all | solution.py:199
  24.8 0.0 copy-start.7
  24.8 0.0 copy-start.1
  24.8 2.7 %collective-permute-start.1 = (f32[2304,128]{1,0:T(8,128)}, f32[2304,128]{1,0:T(8,128)}, u32[]{:S(2)}, u32[]{:S(2)}) collective-permute-start(f32[2304,128]{1,0:T(8,128)} %app_own.1), channel_id=1, source_target_pairs={{0,1},{1,0},{2,3},{3,2},{4,5},{5,4},{6,7},{7,6},{8,9},{9,8},{10,11... | collective-permute-start | bytes 3538952 | tf_op jit(solution)/shard_map/ppermute | solution.py:181
  27.5 0.0 copy-done.3
  27.5 1.9 %collective-permute-start.2 = (f32[2304,128]{1,0:T(8,128)S(1)}, f32[2304,128]{1,0:T(8,128)}, u32[]{:S(2)}, u32[]{:S(2)}) collective-permute-start(f32[2304,128]{1,0:T(8,128)S(1)} %copy-done.3), channel_id=1, source_target_pairs={{0,1},{1,0},{2,3},{3,2},{4,5},{5,4},{6,7},{7,6},{8,9},{9,8},{10,11... | collective-permute-start | bytes 3538952 | tf_op jit(solution)/shard_map/ppermute | solution.py:182
  29.5 4.7 %all-to-all-done.parts_ref = f32[32,8,128]{2,1,0:T(8,128)} async-done(((f32[32,8,128]{2,1,0:T(8,128)}), f32[32,8,128]{2,1,0:T(8,128)}, u32[]{:S(2)}, u32[]{:S(2)}) %all-to-all-start) | async-done | bytes 131104 | tf_op jit(solution)/shard_map/all_to_all | solution.py:199
  34.1 1.7 %spread.1 = f32[16,40,128]{2,1,0:T(8,128)} custom-call(f32[32,8,128]{2,1,0:T(8,128)} %all-to-all-done.parts_ref, f32[32,128]{1,0:T(8,128)} %panel_ref.1), custom_call_target="tpu_custom_call" | custom-call | tf_op jit(solution)/shard_map/spread/pallas_call | solution.py:201
  35.8 22.4 %all_to_all.15 = f32[16,40,128]{2,1,0:T(8,128)} all-to-all(f32[16,40,128]{2,1,0:T(8,128)} %spread.1), channel_id=1, replica_groups=mesh['space'=32,'brow'=8,'bcol'=2] {'brow','bcol'}, dimensions={0} | all-to-all | bytes 655360 | tf_op jit(solution)/shard_map/all_to_all | solution.py:208
  58.2 1.7 %gather.1 = f32[32,16,128]{2,1,0:T(8,128)} custom-call(f32[8,2,40,128]{3,2,1,0:T(8,128)} %bitcast.5), custom_call_target="tpu_custom_call" | custom-call | tf_op jit(solution)/shard_map/gather/pallas_call | solution.py:210
  59.9 4.6 %all-to-all-start.2 = ((f32[32,16,128]{2,1,0:T(8,128)}), f32[32,16,128]{2,1,0:T(8,128)}, u32[]{:S(2)}, u32[]{:S(2)}) async-start(f32[32,16,128]{2,1,0:T(8,128)} %gather.1), calls=%async_computation.2 | async-start | bytes 524288 | tf_op jit(solution)/shard_map/all_to_all | solution.py:217
  64.5 0.0 copy-done.7
  64.5 0.8 copy.6.col_ref
  65.3 0.0 collective-permute-done.1.app_oth
  65.3 0.0 collective-permute-done.2.cot_oth
  65.3 11.9 %all-to-all-done.2.sums_ref = f32[32,16,128]{2,1,0:T(8,128)} async-done(((f32[32,16,128]{2,1,0:T(8,128)}), f32[32,16,128]{2,1,0:T(8,128)}, u32[]{:S(2)}, u32[]{:S(2)}) %all-to-all-start.2) | async-done | bytes 262176 | tf_op jit(solution)/shard_map/all_to_all | solution.py:217
  77.2 0.0 copy-done.1
  77.2 0.0 copy-start.4
  77.2 1.0 %copy-done.4 = f32[16,40,128]{2,1,0:T(8,128)S(1)} copy-done((f32[16,40,128]{2,1,0:T(8,128)S(1)}, f32[16,40,128]{2,1,0:T(8,128)}, u32[]{:S(2)}) %copy-start.4) | copy-done | bytes 327704
  78.2 0.0 copy-start.5
  78.2 1.3 %copy-done.5 = f32[2304,128]{1,0:T(8,128)S(1)} copy-done((f32[2304,128]{1,0:T(8,128)S(1)}, f32[2304,128]{1,0:T(8,128)}, u32[]{:S(2)}) %copy-start.5) | copy-done | bytes 1179672
  79.4 0.0 copy-start.6
  79.4 0.9 %copy-done.6 = f32[256,1]{1,0:T(8,128)S(1)} copy-done((f32[256,1]{1,0:T(8,128)S(1)}, f32[256,1]{1,0:T(8,128)}, u32[]{:S(2)}) %copy-start.6) | copy-done | bytes 1048
  80.3 7.6 %tail.1 = f32[2304,128]{1,0:T(8,128)} custom-call(s32[1]{0:T(128)} %bitcast.bcol_ref, f32[32,16,128]{2,1,0:T(8,128)} %all-to-all-done.2.sums_ref, f32[8,2,40,128]{3,2,1,0:T(8,128)S(1)} %bitcast.6, f32[1,256]{1,0:T(1,128)S(1)} %bitcast.8, f32[256,1]{1,0:T(8,128)S(1)} %copy-done.6, f32[2304,128]{1,0:T(8,128)S(1)} %copy-done.1, ...), custom_call_target="tpu_custom_call" | custom-call | tf_op jit(solution)/shard_map/tail/pallas_call | solution.py:219
Async XLA Ops:
  0.0 11.4 %collective-permute-start = (f32[2304,128]{1,0:T(8,128)}, f32[2304,128]{1,0:T(8,128)S(1)}, u32[]{:S(2)}, u32[]{:S(2)}) collective-permute-start(f32[2304,128]{1,0:T(8,128)} %orb_own.1), channel_id=1, source_target_pairs={{0,1},{1,0},{2,3},{3,2},{4,5},{5,4},{6,7},{7,6},{8,9},{9,8},{10,11... | collective-permute-start | bytes 3538952 | tf_op jit(solution)/shard_map/ppermute | solution.py:180
  11.4 1.3 %copy-start = (f32[2304,128]{1,0:T(8,128)S(1)}, f32[2304,128]{1,0:T(8,128)}, u32[]{:S(2)}) copy-start(f32[2304,128]{1,0:T(8,128)} %orb_own.1) | copy-start | bytes 3538948
  12.7 1.3 %copy-start.2 = (f32[2304,128]{1,0:T(8,128)S(1)}, f32[2304,128]{1,0:T(8,128)}, u32[]{:S(2)}) copy-start(f32[2304,128]{1,0:T(8,128)} %cot_own.1) | copy-start | bytes 3538948
  14.0 13.5 %copy-start.3 = (f32[2304,128]{1,0:T(8,128)S(1)}, f32[2304,128]{1,0:T(8,128)}, u32[]{:S(2)}) copy-start(f32[2304,128]{1,0:T(8,128)} %cot_own.1) | copy-start | bytes 3538948
  17.1 17.0 %all-to-all-start = ((f32[32,8,128]{2,1,0:T(8,128)}), f32[32,8,128]{2,1,0:T(8,128)}, u32[]{:S(2)}, u32[]{:S(2)}) async-start(f32[32,8,128]{2,1,0:T(8,128)} %bitcast.1), calls=%async_computation | async-start | bytes 262144 | tf_op jit(solution)/shard_map/all_to_all | solution.py:199
  24.8 39.7 %copy-start.7 = (f32[256]{0:T(256)S(1)}, f32[256]{0:T(256)}, u32[]{:S(2)}) copy-start(f32[256]{0:T(256)} %param.9) | copy-start | bytes 3076
  24.8 52.4 %copy-start.1 = (f32[2304,128]{1,0:T(8,128)S(1)}, f32[2304,128]{1,0:T(8,128)}, u32[]{:S(2)}) copy-start(f32[2304,128]{1,0:T(8,128)} %orb_own.1) | copy-start | bytes 3538948
  24.8 40.5 %collective-permute-start.1 = (f32[2304,128]{1,0:T(8,128)}, f32[2304,128]{1,0:T(8,128)}, u32[]{:S(2)}, u32[]{:S(2)}) collective-permute-start(f32[2304,128]{1,0:T(8,128)} %app_own.1), channel_id=1, source_target_pairs={{0,1},{1,0},{2,3},{3,2},{4,5},{5,4},{6,7},{7,6},{8,9},{9,8},{10,11... | collective-permute-start | bytes 3538952 | tf_op jit(solution)/shard_map/ppermute | solution.py:181
  27.5 37.7 %collective-permute-start.2 = (f32[2304,128]{1,0:T(8,128)S(1)}, f32[2304,128]{1,0:T(8,128)}, u32[]{:S(2)}, u32[]{:S(2)}) collective-permute-start(f32[2304,128]{1,0:T(8,128)S(1)} %copy-done.3), channel_id=1, source_target_pairs={{0,1},{1,0},{2,3},{3,2},{4,5},{5,4},{6,7},{7,6},{8,9},{9,8},{10,11... | collective-permute-start | bytes 3538952 | tf_op jit(solution)/shard_map/ppermute | solution.py:182
  59.9 17.3 %all-to-all-start.2 = ((f32[32,16,128]{2,1,0:T(8,128)}), f32[32,16,128]{2,1,0:T(8,128)}, u32[]{:S(2)}, u32[]{:S(2)}) async-start(f32[32,16,128]{2,1,0:T(8,128)} %gather.1), calls=%async_computation.2 | async-start | bytes 524288 | tf_op jit(solution)/shard_map/all_to_all | solution.py:217
  77.2 1.0 %copy-start.4 = (f32[16,40,128]{2,1,0:T(8,128)S(1)}, f32[16,40,128]{2,1,0:T(8,128)}, u32[]{:S(2)}) copy-start(f32[16,40,128]{2,1,0:T(8,128)} %all_to_all.15) | copy-start | bytes 983044
  78.2 1.3 %copy-start.5 = (f32[2304,128]{1,0:T(8,128)S(1)}, f32[2304,128]{1,0:T(8,128)}, u32[]{:S(2)}) copy-start(f32[2304,128]{1,0:T(8,128)} %app_own.1) | copy-start | bytes 3538948
  79.4 0.9 %copy-start.6 = (f32[256,1]{1,0:T(8,128)S(1)}, f32[256,1]{1,0:T(8,128)}, u32[]{:S(2)}) copy-start(f32[256,1]{1,0:T(8,128)} %copy.6.col_ref) | copy-start | bytes 3076

commit v2 on v0

v2 whole, which is shorter than its diff:
```python
import jax
import jax.numpy as jnp
from jax import lax
from jax.experimental import pallas as pl
from jax.experimental.pallas import tpu as pltpu
from jax.sharding import PartitionSpec as P

F32 = jnp.float32
BF16 = jnp.bfloat16
VMEM = pl.BlockSpec(memory_space=pltpu.VMEM)
SMEM = pl.BlockSpec(memory_space=pltpu.SMEM)
HBM = pl.BlockSpec(memory_space=pltpu.HBM)
GRAM_CHUNK = 1152
TAIL_CHUNK = 1152
INNER = ((1,), (0,))
MIB = 2**20


def dot(left, right, dims=INNER, precision=None):
    return lax.dot_general(
        left, right, (dims, ((), ())), preferred_element_type=F32, precision=precision
    )


def split(x):
    high = x.astype(BF16)
    return high, (x - high.astype(F32)).astype(BF16)


def product(left, right, dims=INNER):
    return dot(left[0], right[0], dims) + (dot(left[1], right[0], dims) + dot(left[0], right[1], dims))


def halves(x, axis):
    return jnp.concatenate(split(x), axis=axis)


def folded(total):
    rows, columns = total.shape[0] // 2, total.shape[1] // 2
    top, bottom = total[:rows], total[rows:]
    return (top[:, :columns] + top[:, columns:]) + (bottom[:, :columns] + bottom[:, columns:])


def own_kernel(
    orb_hbm, app_hbm, cot_hbm, out_ref, cot_t_ref, orb, pair, sems
):
    cells = orb.shape[0]
    steps = cot_t_ref.shape[0]
    chunk = cells // steps
    copies = []
    for step in range(steps):
        rows = pl.ds(step * chunk, chunk)
        below = pl.ds(cells + step * chunk, chunk)
        group = [
            pltpu.make_async_copy(orb_hbm.at[rows], orb.at[rows], sems.at[step, 0]),
            pltpu.make_async_copy(cot_hbm.at[rows], pair.at[below], sems.at[step, 1]),
        ]
        for copy in group:
            copy.start()
        copies.append(group)
    last = pltpu.make_async_copy(app_hbm, pair.at[pl.ds(0, cells)], sems.at[steps, 0])
    last.start()
    total = None
    for step in range(steps):
        for copy in copies[step]:
            copy.wait()
        cot_t = halves(pair[pl.ds(cells + step * chunk, chunk), :].T, 0)
        cot_t_ref[step] = cot_t
        part = dot(cot_t, halves(orb[pl.ds(step * chunk, chunk), :], 1))
        total = part if total is None else total + part
    out_ref[...] = folded(total)
    last.wait()


def other_kernel(bcol_ref, own_ref, cot_t_ref, orb_ref, out_ref):
    steps = cot_t_ref.shape[0]
    chunk = orb_ref.shape[0] // steps
    width = own_ref.shape[0]
    total = None
    for step in range(steps):
        part = dot(cot_t_ref[step], halves(orb_ref[pl.ds(step * chunk, chunk), :], 1))
        total = part if total is None else total + part
    mine = bcol_ref[0]
    out_ref[pl.ds(pl.multiple_of(mine * width, width), width), :] = own_ref[...]
    out_ref[pl.ds(pl.multiple_of((1 - mine) * width, width), width), :] = folded(total)


def spread_kernel(parts_ref, panel_ref, out_ref):
    both = jnp.concatenate([jnp.sum(parts_ref[...], axis=0), panel_ref[...]], axis=0)
    out_ref[...] = jnp.broadcast_to(both[None], out_ref.shape)


def gather_kernel(parts_ref, out_ref, columns_ref):
    tile = out_ref.shape[1]
    out_ref[...] = jnp.broadcast_to(jnp.sum(parts_ref[:, :tile, :], axis=0)[None], out_ref.shape)
    columns_ref[...] = parts_ref[:, tile:, :].reshape(columns_ref.shape)


def join_kernel(sums_ref, columns_ref, out_ref):
    rows = sums_ref.shape[0]
    out_ref[:rows, :] = sums_ref[...]
    out_ref[rows:, :] = columns_ref[...]


def tail_kernel(
    bcol_ref, whole_ref, row_ref, orb, pair, orb_oth, pair_oth, out_hbm, result, weights, sems
):
    cells, width = result.shape
    steps = sems.shape[0]
    chunk = cells // steps
    mine = bcol_ref[0]
    bands = 2 * width
    first = pl.ds(pl.multiple_of(mine * width, width), width)
    second = pl.ds(pl.multiple_of((1 - mine) * width, width), width)
    grad_t = jnp.concatenate(
        [
            jnp.concatenate(
                [whole_ref[b * width : (b + 1) * width, c * width : (c + 1) * width] for b in range(2)],
                axis=1,
            )
            for c in range(2)
        ],
        axis=0,
    )
    rotation = split(whole_ref[bands:, :])
    gram_t = product(split(grad_t), rotation)
    at_row = lax.broadcasted_iota(jnp.int32, (bands, bands), 0)
    at_col = lax.broadcasted_iota(jnp.int32, (bands, bands), 1)
    diagonal = at_row == at_col
    levels_row = jnp.broadcast_to(row_ref[...], (bands, bands))
    levels_col = levels_row.T
    gaps = jnp.where(diagonal, 1.0, levels_col - levels_row)
    mixing_t = jnp.where(diagonal, 0.0, (1.0 / gaps) * gram_t)
    sym_ham = mixing_t + mixing_t.T
    scaled = levels_col * mixing_t
    sym_ovl = scaled + scaled.T + jnp.where(diagonal, gram_t, 0.0)
    rot_rows = whole_ref[pl.ds(pl.multiple_of(bands + mine * width, width), width), :]
    right = product(
        split(jnp.concatenate([sym_ovl, sym_ham], axis=0)), split(rot_rows), ((1,), (1,))
    )
    coefs = product(rotation, split(jnp.concatenate([-right[:bands], right[bands:]], axis=1)))
    for at, block in enumerate((coefs[:, :width], coefs[:, width:], rot_rows.T)):
        weights[at] = halves(block, 1)
    weight = jnp.concatenate(
        [weights[at, rows, :] for at in range(3) for rows in (first, second)], axis=0
    )
    outs = []
    for step in range(steps):
        rows = pl.ds(step * chunk, chunk)
        below = pl.ds(cells + step * chunk, chunk)
        left = jnp.concatenate(
            [
                orb[rows, :],
                orb_oth[rows, :],
                pair[rows, :],
                pair_oth[rows, :],
                pair[below, :],
                pair_oth[below, :],
            ],
            axis=1,
        )
        high, low = split(left)
        wide = dot(high, weight)
        result[rows, :] = wide[:, :width] + wide[:, width:] + dot(low, weight[:, :width])
        copy = pltpu.make_async_copy(result.at[rows], out_hbm.at[rows], sems.at[step])
        copy.start()
        outs.append(copy)
    for copy in outs:
        copy.wait()


def limit(mib):
    return pltpu.CompilerParams(vmem_limit_bytes=mib * MIB)


def own_gram(orbitals, applied, cotangent):
    cells, width = orbitals.shape
    steps = cells // GRAM_CHUNK
    return pl.pallas_call(
        own_kernel,
        out_shape=(
            jax.ShapeDtypeStruct((width, width), F32),
            jax.ShapeDtypeStruct((steps, 2 * width, GRAM_CHUNK), BF16),
            jax.ShapeDtypeStruct((cells, width), F32),
            jax.ShapeDtypeStruct((2 * cells, width), F32),
        ),
        in_specs=[HBM] * 3,
        out_specs=(VMEM,) * 4,
        scratch_shapes=[pltpu.SemaphoreType.DMA((steps + 1, 2))],
        compiler_params=limit(12),
        cost_estimate=pl.CostEstimate(
            flops=8 * cells * width * width, bytes_accessed=3 * 4 * cells * width, transcendentals=0
        ),
        name="own_gram",
    )(orbitals, applied, cotangent)


def whole_gram(mine, own, cot_t, orb_oth):
    cells, width = orb_oth.shape
    return pl.pallas_call(
        other_kernel,
        out_shape=jax.ShapeDtypeStruct((2 * width, width), F32),
        in_specs=[SMEM, VMEM, VMEM, VMEM],
        out_specs=VMEM,
        compiler_params=limit(10),
        name="whole_gram",
    )(mine, own, cot_t, orb_oth)


def spread(parts, panel, receivers):
    space, tile, width = parts.shape
    return pl.pallas_call(
        spread_kernel,
        out_shape=jax.ShapeDtypeStruct((receivers, tile + panel.shape[0], width), F32),
        in_specs=[VMEM, VMEM],
        out_specs=VMEM,
        compiler_params=limit(2),
        name="spread",
    )(parts, panel)


def gather(panels, space, tile):
    brow, rows, width = panels.shape
    return pl.pallas_call(
        gather_kernel,
        out_shape=(
            jax.ShapeDtypeStruct((space, tile, width), F32),
            jax.ShapeDtypeStruct((brow * (rows - tile), width), F32),
        ),
        in_specs=[VMEM],
        out_specs=(VMEM, VMEM),
        compiler_params=limit(2),
        name="gather",
    )(panels)


def join(sums, columns):
    rows, width = sums.shape
    return pl.pallas_call(
        join_kernel,
        out_shape=jax.ShapeDtypeStruct((2 * rows, width), F32),
        in_specs=[VMEM, VMEM],
        out_specs=VMEM,
        compiler_params=limit(2),
        name="join",
    )(sums, columns)


def tail(mine, whole, levels, orb, pair, orb_oth, pair_oth):
    cells, width = orb.shape
    bands = 2 * width
    steps = cells // TAIL_CHUNK
    return pl.pallas_call(
        tail_kernel,
        out_shape=jax.ShapeDtypeStruct((cells, width), F32),
        in_specs=[SMEM] + [VMEM] * 6,
        out_specs=HBM,
        scratch_shapes=[
            pltpu.VMEM((cells, width), F32),
            pltpu.VMEM((3, bands, bands), BF16),
            pltpu.SemaphoreType.DMA((steps,)),
        ],
        compiler_params=limit(20),
        name="tail",
    )(mine, whole, levels.reshape(1, bands), orb, pair, orb_oth, pair_oth)


def body(orbitals, applied, cotangent, panel, levels):
    width = orbitals.shape[1]
    swap = [(0, 1), (1, 0)]
    space = lax.axis_size("space")
    brow = lax.axis_size("brow")
    tile = 2 * width // space
    mine = lax.axis_index("bcol").reshape(1)

    blocks = [pltpu.with_memory_space_constraint(x, pltpu.HBM) for x in (orbitals, applied, cotangent)]
    orb_oth = lax.ppermute(orbitals, "bcol", swap)
    own, cot_t, orb, pair = own_gram(*blocks)
    partial = whole_gram(mine, own, cot_t, orb_oth)
    pair, partial = lax.optimization_barrier((pair, partial))
    pair_oth = lax.ppermute(pair, "bcol", swap)
    parts = lax.all_to_all(partial.reshape(space, tile, width), "space", 0, 0, tiled=True)
    panels = lax.all_to_all(spread(parts, panel, brow), "brow", 0, 0, tiled=True)
    tiles, columns = gather(panels, space, tile)
    sums = lax.all_to_all(tiles, "space", 0, 0, tiled=True).reshape(2 * width, width)
    whole = lax.all_gather(join(sums, columns), "bcol", axis=1, tiled=True)
    return tail(mine, whole, levels, orb, pair, orb_oth, pair_oth)


def solution(mesh):
    return jax.shard_map(
        body,
        mesh=mesh,
        in_specs=(
            P(("space", "brow"), "bcol"),
            P(("space", "brow"), "bcol"),
            P(("space", "brow"), "bcol"),
            P("brow", "bcol"),
            P(),
        ),
        out_specs=P(("space", "brow"), "bcol"),
        check_vma=False,
    )
```

time: 324 us -> 69.5 us (0.21)
  waiting for transfers between devices: 252 us -> 0.42 us
  matrix products: 20.4 us -> 0 us
  blocking collectives: 33.7 us -> 50.8 us
  between operations: 13.2 us -> 0.05 us
  starting transfers between devices: 0.12 us -> 11.1 us
  Pallas kernels: 0 us -> 6.92 us
  local copies, waits for them, and re-layouts: 4.21 us -> 0.01 us
    psum x1 -> x0, waiting for transfers between devices: 197 us -> none  [band_plan(): col_sums = lax.psum(inner_cells(orb_whole, cotangent), ('space', 'brow'))]
    all_gather x3 -> x0, waiting for transfers between devices: 53.2 us -> none  [the longest x1 27.9 us: band_plan(): orb_whole = lax.all_gather(orbitals, 'bcol', axis=1, tiled=True)]
    all_to_all x0 -> x3, blocking collectives: none -> 44.8 us  [the longest x1 17.1 us: body(): lax.all_to_all(partial.reshape(space, tile, width), 'space', 0, 0, tiled=...]
    all_gather x3 -> x1, blocking collectives: 33.7 us -> 6.05 us  [body(): whole = lax.all_gather(join(sums, columns), 'bcol', axis=1, tiled=True)]
    dot_general x9 -> x0, matrix products: 20.4 us -> none  [the longest x4 8.33 us: matmul(): jnp.dot(left, right, preferred_element_type=jnp.float32, precision=lax.Pr...]
    ppermute x0 -> x2, starting transfers between devices: none -> 11.1 us  [the longest x1 8.77 us: body(): orb_oth = lax.ppermute(orbitals, 'bcol', swap)]
    pallas_call x0 -> x6, Pallas kernels: none -> 6.92 us  [the longest x1 4.12 us: tail(): pl.pallas_call(tail_kernel, out_shape=jax.ShapeDtypeStruct((cells, width)...]
  transfers between devices with their start and end apart: 4 -> 2, of which waited for: 4 -> 1; matrix products, arithmetic and copies ran while one was open for 4% -> 0% of each run, Pallas kernels for 0% -> 3%
where the time goes in v2:
time: 69.5 us; the launch traced here: 69.3 us
  blocking collectives  50.8 us (73%)
  starting transfers between devices  11.1 us (16%)
  Pallas kernels  6.92 us (10%)
    all_to_all x1, blocking collectives, body(): lax.all_to_all(partial.reshape(space, tile, width), 'space', 0, 0, tiled=...  17.1 us
    all_to_all x1, blocking collectives, body(): lax.all_to_all(spread(parts, panel, brow), 'brow', 0, 0, tiled=True)  14.9 us
    all_to_all x1, blocking collectives, body(): lax.all_to_all(tiles, 'space', 0, 0, tiled=True).reshape(2 * width, width)  12.7 us
    ppermute x1, starting transfers between devices, body(): orb_oth = lax.ppermute(orbitals, 'bcol', swap)  8.77 us
    all_gather x1, blocking collectives, body(): whole = lax.all_gather(join(sums, columns), 'bcol', axis=1, tiled=True)  6.05 us
    pallas_call x1, Pallas kernels, tail(): pl.pallas_call(tail_kernel, out_shape=jax.ShapeDtypeStruct((cells, width)...  4.12 us
    ppermute x1, starting transfers between devices, body(): pair_oth = lax.ppermute(pair, 'bcol', swap)  2.28 us
    pallas_call x1, Pallas kernels, own_gram(): pl.pallas_call(own_kernel, out_shape=(jax.ShapeDtypeStruct((width, width)...  2.23 us
  transfers between devices with their start and end apart: 2, of which 1 were waited for; matrix products, arithmetic and copies ran while one was open for 0% of the time, Pallas kernels for 3%

profile of v2, /device:TPU:1, one launch (start us, length us, event | category | flops | bytes accessed | tf_op | source)
XLA Modules:
  0.0 69.3 jit_solution(1952284317053335990)
XLA Ops:
  0.0 8.8 %collective-permute-start = (f32[2304,128]{1,0:T(8,128)}, f32[2304,128]{1,0:T(8,128)S(1)}, u32[]{:S(2)}, u32[]{:S(2)}) collective-permute-start(f32[2304,128]{1,0:T(8,128)} %orb_hbm.1), channel_id=1, source_target_pairs={{0,1},{1,0},{2,3},{3,2},{4,5},{5,4},{6,7},{7,6},{8,9},{9,8},{10,11... | collective-permute-start | bytes 3538952 | tf_op jit(solution)/shard_map/ppermute | solution.py:277
  8.8 2.2 %own_gram.1 = (f32[128,128]{1,0:T(8,128)S(1)}, bf16[2,256,1152]{2,1,0:T(8,128)(2,1)S(1)}, f32[2304,128]{1,0:T(8,128)S(1)}, f32[4608,128]{1,0:T(8,128)S(1)}) custom-call(f32[2304,128]{1,0:T(8,128)} %orb_hbm.1, f32[2304,128]{1,0:T(8,128)} %app_hbm.1, f32[2304,128]{1,0:T(8,128)} %cot_hbm.1), custom_call_target="tpu_custom_call" | custom-call | flops 301989888 | bytes 3538944 | tf_op jit(solution)/shard_map/own_gram/pallas_call | solution.py:179
  11.0 0.4 collective-permute-done.orb_ref.orb_oth
  11.4 0.0 copy-start
  11.4 0.5 whole_gram.1
  12.0 2.3 %collective-permute-start.1 = (f32[4608,128]{1,0:T(8,128)S(1)}, f32[4608,128]{1,0:T(8,128)S(1)}, u32[]{:S(2)}, u32[]{:S(2)}) collective-permute-start(f32[4608,128]{1,0:T(8,128)S(1)} %get-tuple-element.20.pair), channel_id=1, source_target_pairs={{0,1},{1,0},{2,3},{3,2},{4,5},{5,4},{6,7},{7,6},{8,9},{9,8},{10,11... | collective-permute-start | bytes 7077896 | tf_op jit(solution)/shard_map/ppermute | solution.py:281
  14.2 17.1 %all_to_all.15.parts_ref = f32[32,8,128]{2,1,0:T(8,128)S(1)} all-to-all(f32[32,8,128]{2,1,0:T(8,128)S(1)} %bitcast.4), channel_id=1, replica_groups=mesh['space'=32,'brow'=8,'bcol'=2] {'space'}, dimensions={0} | all-to-all | bytes 262144 | tf_op jit(solution)/shard_map/all_to_all | solution.py:282
  31.4 0.0 copy-done
  31.4 0.0 copy-start.1
  31.4 14.9 %all_to_all.16.parts_ref = f32[8,40,128]{2,1,0:T(8,128)S(1)} all-to-all(f32[8,40,128]{2,1,0:T(8,128)S(1)} %spread.1), channel_id=1, replica_groups=mesh['space'=32,'brow'=8,'bcol'=2] {'brow'}, dimensions={0} | all-to-all | bytes 327680 | tf_op jit(solution)/shard_map/all_to_all | solution.py:283
  46.4 12.7 %all_to_all.17 = f32[32,8,128]{2,1,0:T(8,128)S(1)} all-to-all(f32[32,8,128]{2,1,0:T(8,128)S(1)} %get-tuple-element.17), channel_id=1, replica_groups=mesh['space'=32,'brow'=8,'bcol'=2] {'space'}, dimensions={0} | all-to-all | bytes 262144 | tf_op jit(solution)/shard_map/all_to_all | solution.py:285
  59.1 6.1 %all_gather.3.whole_ref = f32[512,256]{1,0:T(8,128)S(1)} all-gather(f32[512,128]{1,0:T(8,128)S(1)} %join.1), channel_id=1, replica_groups=mesh['space'=32,'brow'=8,'bcol'=2] {'bcol'}, dimensions={1}, use_global_device_ids=true | all-gather | bytes 786432 | tf_op jit(solution)/shard_map/all_gather | solution.py:286
  65.1 0.0 collective-permute-done.1.pair_oth
  65.1 0.0 copy-done.1
  65.1 4.1 %tail.1 = f32[2304,128]{1,0:T(8,128)} custom-call(s32[1]{0:T(128)} %bitcast.bcol_ref, f32[512,256]{1,0:T(8,128)S(1)} %all_gather.3.whole_ref, f32[1,256]{1,0:T(1,128)S(1)} %bitcast.6, f32[2304,128]{1,0:T(8,128)S(1)} %get-tuple-element.19.orb, f32[4608,128]{1,0:T(8,128)S(1)} %get-tuple-element.20.pair, f32[2304,128]{1,0:T(8,128)S(1)} %collective-permute-done.orb_ref.orb_oth, ...), custom_call_target="tpu_custom_call" | custom-call | tf_op jit(solution)/shard_map/tail/pallas_call | solution.py:253
  (3 shorter events, 0.1 us)
Async XLA Ops:
  0.0 11.4 %collective-permute-start = (f32[2304,128]{1,0:T(8,128)}, f32[2304,128]{1,0:T(8,128)S(1)}, u32[]{:S(2)}, u32[]{:S(2)}) collective-permute-start(f32[2304,128]{1,0:T(8,128)} %orb_hbm.1), channel_id=1, source_target_pairs={{0,1},{1,0},{2,3},{3,2},{4,5},{5,4},{6,7},{7,6},{8,9},{9,8},{10,11... | collective-permute-start | bytes 3538952 | tf_op jit(solution)/shard_map/ppermute | solution.py:277
  11.4 19.9 %copy-start = (f32[32,128]{1,0:T(8,128)S(1)}, f32[32,128]{1,0:T(8,128)}, u32[]{:S(2)}) copy-start(f32[32,128]{1,0:T(8,128)} %panel_ref.1) | copy-start | bytes 49156
  12.0 53.2 %collective-permute-start.1 = (f32[4608,128]{1,0:T(8,128)S(1)}, f32[4608,128]{1,0:T(8,128)S(1)}, u32[]{:S(2)}, u32[]{:S(2)}) collective-permute-start(f32[4608,128]{1,0:T(8,128)S(1)} %get-tuple-element.20.pair), channel_id=1, source_target_pairs={{0,1},{1,0},{2,3},{3,2},{4,5},{5,4},{6,7},{7,6},{8,9},{9,8},{10,11... | collective-permute-start | bytes 7077896 | tf_op jit(solution)/shard_map/ppermute | solution.py:281
  31.4 33.8 %copy-start.1 = (f32[256]{0:T(256)S(1)}, f32[256]{0:T(256)}, u32[]{:S(2)}) copy-start(f32[256]{0:T(256)} %param.9) | copy-start | bytes 3076

commit v3 on v2

--- a/solution.py
+++ b/solution.py
@@ -3,16 +3,19 @@
 from jax import lax
 from jax.experimental import pallas as pl
 from jax.experimental.pallas import tpu as pltpu
+from jax.sharding import Mesh
 from jax.sharding import PartitionSpec as P
 
 F32 = jnp.float32
 BF16 = jnp.bfloat16
 VMEM = pl.BlockSpec(memory_space=pltpu.VMEM)
-SMEM = pl.BlockSpec(memory_space=pltpu.SMEM)
 HBM = pl.BlockSpec(memory_space=pltpu.HBM)
 GRAM_CHUNK = 1152
 TAIL_CHUNK = 1152
 INNER = ((1,), (0,))
+NEAR = ("zn", "x", "yn")
+FAR = ("zf", "yf")
+OCTET = 8
 MIB = 2**20
 
 
@@ -72,7 +75,7 @@
     last.wait()
 
 
-def other_kernel(bcol_ref, own_ref, cot_t_ref, orb_ref, out_ref):
+def other_kernel(own_ref, cot_t_ref, orb_ref, out_ref):
     steps = cot_t_ref.shape[0]
     chunk = orb_ref.shape[0] // steps
     width = own_ref.shape[0]
@@ -80,49 +83,60 @@
     for step in range(steps):
         part = dot(cot_t_ref[step], halves(orb_ref[pl.ds(step * chunk, chunk), :], 1))
         total = part if total is None else total + part
-    mine = bcol_ref[0]
+    mine = lax.axis_index("bcol")
     out_ref[pl.ds(pl.multiple_of(mine * width, width), width), :] = own_ref[...]
     out_ref[pl.ds(pl.multiple_of((1 - mine) * width, width), width), :] = folded(total)
 
 
 def spread_kernel(parts_ref, panel_ref, out_ref):
-    both = jnp.concatenate([jnp.sum(parts_ref[...], axis=0), panel_ref[...]], axis=0)
+    octet = pl.ds(pl.multiple_of(lax.axis_index("x") * OCTET, OCTET), OCTET)
+    both = jnp.concatenate([jnp.sum(parts_ref[...], axis=0), panel_ref[octet, :]], axis=0)
     out_ref[...] = jnp.broadcast_to(both[None], out_ref.shape)
 
 
-def gather_kernel(parts_ref, out_ref, columns_ref):
-    tile = out_ref.shape[1]
-    out_ref[...] = jnp.broadcast_to(jnp.sum(parts_ref[:, :tile, :], axis=0)[None], out_ref.shape)
-    columns_ref[...] = parts_ref[:, tile:, :].reshape(columns_ref.shape)
-
-
-def join_kernel(sums_ref, columns_ref, out_ref):
-    rows = sums_ref.shape[0]
-    out_ref[:rows, :] = sums_ref[...]
-    out_ref[rows:, :] = columns_ref[...]
+def gather_kernel(parts_ref, out_ref):
+    tile = parts_ref.shape[1] - OCTET
+    octets = parts_ref[pl.ds(2 * lax.axis_index("zn"), 2), tile:, :]
+    total = jnp.sum(parts_ref[:, :tile, :], axis=0)
+    both = jnp.concatenate([total, octets.reshape(2 * OCTET, total.shape[1])], axis=0)
+    out_ref[...] = jnp.broadcast_to(both[None], out_ref.shape)
 
 
 def tail_kernel(
-    bcol_ref, whole_ref, row_ref, orb, pair, orb_oth, pair_oth, out_hbm, result, weights, sems
+    whole_ref, row_ref, orb, pair, orb_oth, pair_oth, out_hbm, result, weights, sems
 ):
     cells, width = result.shape
     steps = sems.shape[0]
     chunk = cells // steps
-    mine = bcol_ref[0]
+    mine = lax.axis_index("bcol")
     bands = 2 * width
     first = pl.ds(pl.multiple_of(mine * width, width), width)
     second = pl.ds(pl.multiple_of((1 - mine) * width, width), width)
+    block = 4 * OCTET
+    tile = 2 * OCTET
+    sums = jnp.concatenate(
+        [whole_ref[q * block : q * block + tile, :] for q in range(bands // tile)], axis=0
+    )
+    octets = []
+    for y in range(bands // block):
+        yf, yn = y // 2, y % 2
+        for x in range(block // OCTET):
+            at = (8 * (yf // 2) + 2 * x + yn) * block + tile + (yf % 2) * OCTET
+            octets.append(whole_ref[at : at + OCTET, :])
+    half = len(octets) // 2
+    top, bottom = (jnp.concatenate(part, axis=0) for part in (octets[:half], octets[half:]))
     grad_t = jnp.concatenate(
         [
             jnp.concatenate(
-                [whole_ref[b * width : (b + 1) * width, c * width : (c + 1) * width] for b in range(2)],
+                [sums[b * width : (b + 1) * width, c * width : (c + 1) * width] for b in range(2)],
                 axis=1,
             )
             for c in range(2)
         ],
         axis=0,
     )
-    rotation = split(whole_ref[bands:, :])
+    rotation = split(jnp.concatenate([top, bottom], axis=0))
+    rot_rows = jnp.where(mine == 0, top, bottom)
     gram_t = product(split(grad_t), rotation)
     at_row = lax.broadcasted_iota(jnp.int32, (bands, bands), 0)
     at_col = lax.broadcasted_iota(jnp.int32, (bands, bands), 1)
@@ -134,7 +148,6 @@
     sym_ham = mixing_t + mixing_t.T
     scaled = levels_col * mixing_t
     sym_ovl = scaled + scaled.T + jnp.where(diagonal, gram_t, 0.0)
-    rot_rows = whole_ref[pl.ds(pl.multiple_of(bands + mine * width, width), width), :]
     right = product(
         split(jnp.concatenate([sym_ovl, sym_ham], axis=0)), split(rot_rows), ((1,), (1,))
     )
@@ -195,23 +208,23 @@
     )(orbitals, applied, cotangent)
 
 
-def whole_gram(mine, own, cot_t, orb_oth):
+def whole_gram(own, cot_t, orb_oth):
     cells, width = orb_oth.shape
     return pl.pallas_call(
         other_kernel,
         out_shape=jax.ShapeDtypeStruct((2 * width, width), F32),
-        in_specs=[SMEM, VMEM, VMEM, VMEM],
+        in_specs=[VMEM, VMEM, VMEM],
         out_specs=VMEM,
         compiler_params=limit(10),
         name="whole_gram",
-    )(mine, own, cot_t, orb_oth)
+    )(own, cot_t, orb_oth)
 
 
 def spread(parts, panel, receivers):
-    space, tile, width = parts.shape
+    near, tile, width = parts.shape
     return pl.pallas_call(
         spread_kernel,
-        out_shape=jax.ShapeDtypeStruct((receivers, tile + panel.shape[0], width), F32),
+        out_shape=jax.ShapeDtypeStruct((receivers, tile + OCTET, width), F32),
         in_specs=[VMEM, VMEM],
         out_specs=VMEM,
         compiler_params=limit(2),
@@ -219,41 +232,26 @@
     )(parts, panel)
 
 
-def gather(panels, space, tile):
-    brow, rows, width = panels.shape
+def gather(parts, receivers):
+    far, rows, width = parts.shape
     return pl.pallas_call(
         gather_kernel,
-        out_shape=(
-            jax.ShapeDtypeStruct((space, tile, width), F32),
-            jax.ShapeDtypeStruct((brow * (rows - tile), width), F32),
-        ),
+        out_shape=jax.ShapeDtypeStruct((receivers, rows + OCTET, width), F32),
         in_specs=[VMEM],
-        out_specs=(VMEM, VMEM),
+        out_specs=VMEM,
         compiler_params=limit(2),
         name="gather",
-    )(panels)
-
-
-def join(sums, columns):
-    rows, width = sums.shape
-    return pl.pallas_call(
-        join_kernel,
-        out_shape=jax.ShapeDtypeStruct((2 * rows, width), F32),
-        in_specs=[VMEM, VMEM],
-        out_specs=VMEM,
-        compiler_params=limit(2),
-        name="join",
-    )(sums, columns)
-
-
-def tail(mine, whole, levels, orb, pair, orb_oth, pair_oth):
+    )(parts)
+
+
+def tail(whole, levels, orb, pair, orb_oth, pair_oth):
     cells, width = orb.shape
     bands = 2 * width
     steps = cells // TAIL_CHUNK
     return pl.pallas_call(
         tail_kernel,
         out_shape=jax.ShapeDtypeStruct((cells, width), F32),
-        in_specs=[SMEM] + [VMEM] * 6,
+        in_specs=[VMEM] * 6,
         out_specs=HBM,
         scratch_shapes=[
             pltpu.VMEM((cells, width), F32),
@@ -262,42 +260,35 @@
         ],
         compiler_params=limit(20),
         name="tail",
-    )(mine, whole, levels.reshape(1, bands), orb, pair, orb_oth, pair_oth)
+    )(whole, levels.reshape(1, bands), orb, pair, orb_oth, pair_oth)
 
 
 def body(orbitals, applied, cotangent, panel, levels):
     width = orbitals.shape[1]
     swap = [(0, 1), (1, 0)]
-    space = lax.axis_size("space")
-    brow = lax.axis_size("brow")
-    tile = 2 * width // space
-    mine = lax.axis_index("bcol").reshape(1)
+    near = lax.axis_size(NEAR)
+    far = lax.axis_size(FAR)
 
     blocks = [pltpu.with_memory_space_constraint(x, pltpu.HBM) for x in (orbitals, applied, cotangent)]
     orb_oth = lax.ppermute(orbitals, "bcol", swap)
     own, cot_t, orb, pair = own_gram(*blocks)
-    partial = whole_gram(mine, own, cot_t, orb_oth)
+    partial = whole_gram(own, cot_t, orb_oth)
     pair, partial = lax.optimization_barrier((pair, partial))
     pair_oth = lax.ppermute(pair, "bcol", swap)
-    parts = lax.all_to_all(partial.reshape(space, tile, width), "space", 0, 0, tiled=True)
-    panels = lax.all_to_all(spread(parts, panel, brow), "brow", 0, 0, tiled=True)
-    tiles, columns = gather(panels, space, tile)
-    sums = lax.all_to_all(tiles, "space", 0, 0, tiled=True).reshape(2 * width, width)
-    whole = lax.all_gather(join(sums, columns), "bcol", axis=1, tiled=True)
-    return tail(mine, whole, levels, orb, pair, orb_oth, pair_oth)
+    parts = lax.all_to_all(partial.reshape(near, -1, width), NEAR, 0, 0, tiled=True)
+    parts = lax.all_to_all(spread(parts, panel, far), FAR, 0, 0, tiled=True)
+    sums = lax.all_to_all(gather(parts, near), NEAR, 0, 0, tiled=True)
+    whole = lax.all_gather(sums.reshape(-1, width), "bcol", axis=1, tiled=True)
+    return tail(whole, levels, orb, pair, orb_oth, pair_oth)
 
 
 def solution(mesh):
+    fine = Mesh(mesh.devices.reshape(4, 2, 4, 4, 2, 2), ("zf", "zn", "x", "yf", "yn", "bcol"))
+    cells = P(("zf", "zn", "x", "yf", "yn"), "bcol")
     return jax.shard_map(
         body,
-        mesh=mesh,
-        in_specs=(
-            P(("space", "brow"), "bcol"),
-            P(("space", "brow"), "bcol"),
-            P(("space", "brow"), "bcol"),
-            P("brow", "bcol"),
-            P(),
-        ),
-        out_specs=P(("space", "brow"), "bcol"),
+        mesh=fine,
+        in_specs=(cells, cells, cells, P(("yf", "yn"), "bcol"), P()),
+        out_specs=cells,
         check_vma=False,
     )

time: 69.5 us -> 66.4 us (0.955)
  blocking collectives: 50.8 us -> 47.6 us
    all_to_all x3, blocking collectives: 44.8 us -> 41.7 us  [the longest x1 23.8 us: body(): parts = lax.all_to_all(spread(parts, panel, far), FAR, 0, 0, tiled=True)]
where the time goes in v3:
time: 66.4 us; the launch traced here: 66.1 us
  blocking collectives  47.6 us (72%)
  starting transfers between devices  11.1 us (17%)
  Pallas kernels  6.93 us (10%)
    all_to_all x1, blocking collectives, body(): parts = lax.all_to_all(spread(parts, panel, far), FAR, 0, 0, tiled=True)  23.8 us
    all_to_all x1, blocking collectives, body(): sums = lax.all_to_all(gather(parts, near), NEAR, 0, 0, tiled=True)  9.27 us
    ppermute x1, starting transfers between devices, body(): orb_oth = lax.ppermute(orbitals, 'bcol', swap)  8.77 us
    all_to_all x1, blocking collectives, body(): lax.all_to_all(partial.reshape(near, -1, width), NEAR, 0, 0, tiled=True)  8.58 us
    all_gather x1, blocking collectives, body(): whole = lax.all_gather(sums.reshape(-1, width), 'bcol', axis=1, tiled=True)  5.95 us
    pallas_call x1, Pallas kernels, tail(): pl.pallas_call(tail_kernel, out_shape=jax.ShapeDtypeStruct((cells, width)...  4.14 us
    ppermute x1, starting transfers between devices, body(): pair_oth = lax.ppermute(pair, 'bcol', swap)  2.28 us
    pallas_call x1, Pallas kernels, own_gram(): pl.pallas_call(own_kernel, out_shape=(jax.ShapeDtypeStruct((width, width)...  2.23 us
  transfers between devices with their start and end apart: 2, of which 1 were waited for; matrix products, arithmetic and copies ran while one was open for 0% of the time, Pallas kernels for 3%

profile of v3, /device:TPU:1, one launch (start us, length us, event | category | flops | bytes accessed | tf_op | source)
XLA Modules:
  0.0 66.1 jit_solution(6201231227909003621)
XLA Ops:
  0.0 8.8 %collective-permute-start = (f32[2304,128]{1,0:T(8,128)}, f32[2304,128]{1,0:T(8,128)S(1)}, u32[]{:S(2)}, u32[]{:S(2)}) collective-permute-start(f32[2304,128]{1,0:T(8,128)} %orb_hbm.1), channel_id=1, source_target_pairs={{0,1},{1,0},{2,3},{3,2},{4,5},{5,4},{6,7},{7,6},{8,9},{9,8},{10,11... | collective-permute-start | bytes 3538952 | tf_op jit(solution)/shard_map/ppermute | solution.py:273
  8.8 2.2 %own_gram.1 = (f32[128,128]{1,0:T(8,128)S(1)}, bf16[2,256,1152]{2,1,0:T(8,128)(2,1)S(1)}, f32[2304,128]{1,0:T(8,128)S(1)}, f32[4608,128]{1,0:T(8,128)S(1)}) custom-call(f32[2304,128]{1,0:T(8,128)} %orb_hbm.1, f32[2304,128]{1,0:T(8,128)} %app_hbm.1, f32[2304,128]{1,0:T(8,128)} %cot_hbm.1), custom_call_target="tpu_custom_call" | custom-call | flops 301989888 | bytes 3538944 | tf_op jit(solution)/shard_map/own_gram/pallas_call | solution.py:192
  11.0 0.4 collective-permute-done.orb_ref.orb_oth
  11.4 0.0 copy-start
  11.4 0.5 whole_gram.1
  12.0 2.3 %collective-permute-start.1 = (f32[4608,128]{1,0:T(8,128)S(1)}, f32[4608,128]{1,0:T(8,128)S(1)}, u32[]{:S(2)}, u32[]{:S(2)}) collective-permute-start(f32[4608,128]{1,0:T(8,128)S(1)} %get-tuple-element.16.pair), channel_id=1, source_target_pairs={{0,1},{1,0},{2,3},{3,2},{4,5},{5,4},{6,7},{7,6},{8,9},{9,8},{10,11... | collective-permute-start | bytes 7077896 | tf_op jit(solution)/shard_map/ppermute | solution.py:277
  14.2 8.6 %all_to_all.15.parts_ref = f32[16,16,128]{2,1,0:T(8,128)S(1)} all-to-all(f32[16,16,128]{2,1,0:T(8,128)S(1)} %bitcast.3), channel_id=1, replica_groups=mesh['zf'=4,'zn'=2,'x'=4,'yf'=4,'yn'=2,'bcol'=2] {'zn','x','yn'}, dimensions={0} | all-to-all | bytes 262144 | tf_op jit(solution)/shard_map/all_to_all | solution.py:278
  22.8 0.0 copy-done
  22.8 0.0 copy-start.1
  22.9 23.8 %all_to_all.16.parts_ref = f32[16,24,128]{2,1,0:T(8,128)S(1)} all-to-all(f32[16,24,128]{2,1,0:T(8,128)S(1)} %spread.1), channel_id=1, replica_groups=mesh['zf'=4,'zn'=2,'x'=4,'yf'=4,'yn'=2,'bcol'=2] {'zf','yf'}, dimensions={0} | all-to-all | bytes 393216 | tf_op jit(solution)/shard_map/all_to_all | solution.py:279
  46.7 9.3 %all_to_all.17 = f32[16,32,128]{2,1,0:T(8,128)S(1)} all-to-all(f32[16,32,128]{2,1,0:T(8,128)S(1)} %gather.1), channel_id=1, replica_groups=mesh['zf'=4,'zn'=2,'x'=4,'yf'=4,'yn'=2,'bcol'=2] {'zn','x','yn'}, dimensions={0} | all-to-all | bytes 524288 | tf_op jit(solution)/shard_map/all_to_all | solution.py:280
  56.0 6.0 %all_gather.3.whole_ref = f32[512,256]{1,0:T(8,128)S(1)} all-gather(f32[512,128]{1,0:T(8,128)S(1)} %bitcast.5), channel_id=1, replica_groups=mesh['zf'=4,'zn'=2,'x'=4,'yf'=4,'yn'=2,'bcol'=2] {'bcol'}, dimensions={1}, use_global_device_ids=true | all-gather | bytes 786432 | tf_op jit(solution)/shard_map/all_gather | solution.py:281
  61.9 0.0 collective-permute-done.1.pair_oth
  61.9 0.0 copy-done.1
  61.9 4.1 %tail.1 = f32[2304,128]{1,0:T(8,128)} custom-call(f32[512,256]{1,0:T(8,128)S(1)} %all_gather.3.whole_ref, f32[1,256]{1,0:T(1,128)S(1)} %bitcast.4, f32[2304,128]{1,0:T(8,128)S(1)} %get-tuple-element.15.orb, f32[4608,128]{1,0:T(8,128)S(1)} %get-tuple-element.16.pair, f32[2304,128]{1,0:T(8,128)S(1)} %collective-permute-done.orb_ref.orb_oth, ...), custom_call_target="tpu_custom_call" | custom-call | tf_op jit(solution)/shard_map/tail/pallas_call | solution.py:251
  (2 shorter events, 0.1 us)
Async XLA Ops:
  0.0 11.4 %collective-permute-start = (f32[2304,128]{1,0:T(8,128)}, f32[2304,128]{1,0:T(8,128)S(1)}, u32[]{:S(2)}, u32[]{:S(2)}) collective-permute-start(f32[2304,128]{1,0:T(8,128)} %orb_hbm.1), channel_id=1, source_target_pairs={{0,1},{1,0},{2,3},{3,2},{4,5},{5,4},{6,7},{7,6},{8,9},{9,8},{10,11... | collective-permute-start | bytes 3538952 | tf_op jit(solution)/shard_map/ppermute | solution.py:273
  11.4 11.4 %copy-start = (f32[32,128]{1,0:T(8,128)S(1)}, f32[32,128]{1,0:T(8,128)}, u32[]{:S(2)}) copy-start(f32[32,128]{1,0:T(8,128)} %panel_ref.1) | copy-start | bytes 49156
  12.0 50.0 %collective-permute-start.1 = (f32[4608,128]{1,0:T(8,128)S(1)}, f32[4608,128]{1,0:T(8,128)S(1)}, u32[]{:S(2)}, u32[]{:S(2)}) collective-permute-start(f32[4608,128]{1,0:T(8,128)S(1)} %get-tuple-element.16.pair), channel_id=1, source_target_pairs={{0,1},{1,0},{2,3},{3,2},{4,5},{5,4},{6,7},{7,6},{8,9},{9,8},{10,11... | collective-permute-start | bytes 7077896 | tf_op jit(solution)/shard_map/ppermute | solution.py:277
  22.8 39.1 %copy-start.1 = (f32[256]{0:T(256)S(1)}, f32[256]{0:T(256)}, u32[]{:S(2)}) copy-start(f32[256]{0:T(256)} %param.9) | copy-start | bytes 3076

commit v4 on v3

--- a/solution.py
+++ b/solution.py
@@ -11,7 +11,7 @@
 VMEM = pl.BlockSpec(memory_space=pltpu.VMEM)
 HBM = pl.BlockSpec(memory_space=pltpu.HBM)
 GRAM_CHUNK = 1152
-TAIL_CHUNK = 1152
+TAIL_CHUNK = 576
 INNER = ((1,), (0,))
 NEAR = ("zn", "x", "yn")
 FAR = ("zf", "yf")
@@ -137,7 +137,18 @@
     )
     rotation = split(jnp.concatenate([top, bottom], axis=0))
     rot_rows = jnp.where(mine == 0, top, bottom)
+    weights[2] = halves(rot_rows.T, 1)
+    weight = jnp.concatenate([weights[2, first, :], weights[2, second, :]], axis=0)
+
+    def rotated(step):
+        below = pl.ds(cells + step * chunk, chunk)
+        high, low = split(jnp.concatenate([pair[below, :], pair_oth[below, :]], axis=1))
+        wide = dot(high, weight)
+        rows = pl.ds(step * chunk, chunk)
+        result[rows, :] = wide[:, :width] + wide[:, width:] + dot(low, weight[:, :width])
+
     gram_t = product(split(grad_t), rotation)
+    rotated(0)
     at_row = lax.broadcasted_iota(jnp.int32, (bands, bands), 0)
     at_col = lax.broadcasted_iota(jnp.int32, (bands, bands), 1)
     diagonal = at_row == at_col
@@ -151,30 +162,24 @@
     right = product(
         split(jnp.concatenate([sym_ovl, sym_ham], axis=0)), split(rot_rows), ((1,), (1,))
     )
+    rotated(1)
     coefs = product(rotation, split(jnp.concatenate([-right[:bands], right[bands:]], axis=1)))
-    for at, block in enumerate((coefs[:, :width], coefs[:, width:], rot_rows.T)):
+    for step in range(2, steps):
+        rotated(step)
+    for at, block in enumerate((coefs[:, :width], coefs[:, width:])):
         weights[at] = halves(block, 1)
     weight = jnp.concatenate(
-        [weights[at, rows, :] for at in range(3) for rows in (first, second)], axis=0
+        [weights[at, rows, :] for at in range(2) for rows in (first, second)], axis=0
     )
     outs = []
     for step in range(steps):
         rows = pl.ds(step * chunk, chunk)
-        below = pl.ds(cells + step * chunk, chunk)
         left = jnp.concatenate(
-            [
-                orb[rows, :],
-                orb_oth[rows, :],
-                pair[rows, :],
-                pair_oth[rows, :],
-                pair[below, :],
-                pair_oth[below, :],
-            ],
-            axis=1,
+            [orb[rows, :], orb_oth[rows, :], pair[rows, :], pair_oth[rows, :]], axis=1
         )
         high, low = split(left)
         wide = dot(high, weight)
-        result[rows, :] = wide[:, :width] + wide[:, width:] + dot(low, weight[:, :width])
+        result[rows, :] += wide[:, :width] + wide[:, width:] + dot(low, weight[:, :width])
         copy = pltpu.make_async_copy(result.at[rows], out_hbm.at[rows], sems.at[step])
         copy.start()
         outs.append(copy)
@@ -272,9 +277,9 @@
     blocks = [pltpu.with_memory_space_constraint(x, pltpu.HBM) for x in (orbitals, applied, cotangent)]
     orb_oth = lax.ppermute(orbitals, "bcol", swap)
     own, cot_t, orb, pair = own_gram(*blocks)
+    pair, own, cot_t = lax.optimization_barrier((pair, own, cot_t))
+    pair_oth = lax.ppermute(pair, "bcol", swap)
     partial = whole_gram(own, cot_t, orb_oth)
-    pair, partial = lax.optimization_barrier((pair, partial))
-    pair_oth = lax.ppermute(pair, "bcol", swap)
     parts = lax.all_to_all(partial.reshape(near, -1, width), NEAR, 0, 0, tiled=True)
     parts = lax.all_to_all(spread(parts, panel, far), FAR, 0, 0, tiled=True)
     sums = lax.all_to_all(gather(parts, near), NEAR, 0, 0, tiled=True)

time: 66.4 us -> 65.3 us (0.983)
  transfers between devices with their start and end apart: 2 -> 2, of which waited for: 1 -> 0; matrix products, arithmetic and copies ran while one was open for 0% -> 0% of each run, Pallas kernels for 3% -> 4%
where the time goes in v4:
time: 65.3 us; the launch traced here: 65 us
  blocking collectives  47.8 us (73%)
  starting transfers between devices  10.7 us (16%)
  Pallas kernels  6.33 us (10%)
    all_to_all x1, blocking collectives, body(): parts = lax.all_to_all(spread(parts, panel, far), FAR, 0, 0, tiled=True)  23.6 us
    all_to_all x1, blocking collectives, body(): sums = lax.all_to_all(gather(parts, near), NEAR, 0, 0, tiled=True)  9.28 us
    ppermute x1, starting transfers between devices, body(): orb_oth = lax.ppermute(orbitals, 'bcol', swap)  8.77 us
    all_to_all x1, blocking collectives, body(): lax.all_to_all(partial.reshape(near, -1, width), NEAR, 0, 0, tiled=True)  8.74 us
    all_gather x1, blocking collectives, body(): whole = lax.all_gather(sums.reshape(-1, width), 'bcol', axis=1, tiled=True)  6.22 us
    pallas_call x1, Pallas kernels, tail(): pl.pallas_call(tail_kernel, out_shape=jax.ShapeDtypeStruct((cells, width)...  3.54 us
    pallas_call x1, Pallas kernels, own_gram(): pl.pallas_call(own_kernel, out_shape=(jax.ShapeDtypeStruct((width, width)...  2.23 us
    ppermute x1, starting transfers between devices, body(): pair_oth = lax.ppermute(pair, 'bcol', swap)  1.92 us
  transfers between devices with their start and end apart: 2, of which 0 were waited for; matrix products, arithmetic and copies ran while one was open for 0% of the time, Pallas kernels for 4%

profile of v4, /device:TPU:1, one launch (start us, length us, event | category | flops | bytes accessed | tf_op | source)
XLA Modules:
  0.0 65.0 jit_solution(707913191808720351)
XLA Ops:
  0.0 8.8 %collective-permute-start = (f32[2304,128]{1,0:T(8,128)}, f32[2304,128]{1,0:T(8,128)S(1)}, u32[]{:S(2)}, u32[]{:S(2)}) collective-permute-start(f32[2304,128]{1,0:T(8,128)} %orb_hbm.1), channel_id=1, source_target_pairs={{0,1},{1,0},{2,3},{3,2},{4,5},{5,4},{6,7},{7,6},{8,9},{9,8},{10,11... | collective-permute-start | bytes 3538952 | tf_op jit(solution)/shard_map/ppermute | solution.py:278
  8.8 2.2 %own_gram.1 = (f32[128,128]{1,0:T(8,128)S(1)}, bf16[2,256,1152]{2,1,0:T(8,128)(2,1)S(1)}, f32[2304,128]{1,0:T(8,128)S(1)}, f32[4608,128]{1,0:T(8,128)S(1)}) custom-call(f32[2304,128]{1,0:T(8,128)} %orb_hbm.1, f32[2304,128]{1,0:T(8,128)} %app_hbm.1, f32[2304,128]{1,0:T(8,128)} %cot_hbm.1), custom_call_target="tpu_custom_call" | custom-call | flops 301989888 | bytes 3538944 | tf_op jit(solution)/shard_map/own_gram/pallas_call | solution.py:197
  11.0 0.0 copy-start
  11.0 1.9 %collective-permute-start.1 = (f32[4608,128]{1,0:T(8,128)S(1)}, f32[4608,128]{1,0:T(8,128)S(1)}, u32[]{:S(2)}, u32[]{:S(2)}) collective-permute-start(f32[4608,128]{1,0:T(8,128)S(1)} %get-tuple-element.18.pair), channel_id=1, source_target_pairs={{0,1},{1,0},{2,3},{3,2},{4,5},{5,4},{6,7},{7,6},{8,9},{9,8},{10,11... | collective-permute-start | bytes 7077896 | tf_op jit(solution)/shard_map/ppermute | solution.py:281
  13.0 0.0 collective-permute-done.orb_ref.orb_oth
  13.0 0.5 whole_gram.1
  13.5 8.7 %all_to_all.15.parts_ref = f32[16,16,128]{2,1,0:T(8,128)S(1)} all-to-all(f32[16,16,128]{2,1,0:T(8,128)S(1)} %bitcast.3), channel_id=1, replica_groups=mesh['zf'=4,'zn'=2,'x'=4,'yf'=4,'yn'=2,'bcol'=2] {'zn','x','yn'}, dimensions={0} | all-to-all | bytes 262144 | tf_op jit(solution)/shard_map/all_to_all | solution.py:283
  22.2 0.0 copy-done
  22.2 0.0 copy-start.1
  22.3 23.6 %all_to_all.16.parts_ref = f32[16,24,128]{2,1,0:T(8,128)S(1)} all-to-all(f32[16,24,128]{2,1,0:T(8,128)S(1)} %spread.1), channel_id=1, replica_groups=mesh['zf'=4,'zn'=2,'x'=4,'yf'=4,'yn'=2,'bcol'=2] {'zf','yf'}, dimensions={0} | all-to-all | bytes 393216 | tf_op jit(solution)/shard_map/all_to_all | solution.py:284
  45.9 9.3 %all_to_all.17 = f32[16,32,128]{2,1,0:T(8,128)S(1)} all-to-all(f32[16,32,128]{2,1,0:T(8,128)S(1)} %gather.1), channel_id=1, replica_groups=mesh['zf'=4,'zn'=2,'x'=4,'yf'=4,'yn'=2,'bcol'=2] {'zn','x','yn'}, dimensions={0} | all-to-all | bytes 524288 | tf_op jit(solution)/shard_map/all_to_all | solution.py:285
  55.2 6.2 %all_gather.3.whole_ref = f32[512,256]{1,0:T(8,128)S(1)} all-gather(f32[512,128]{1,0:T(8,128)S(1)} %bitcast.5), channel_id=1, replica_groups=mesh['zf'=4,'zn'=2,'x'=4,'yf'=4,'yn'=2,'bcol'=2] {'bcol'}, dimensions={1}, use_global_device_ids=true | all-gather | bytes 786432 | tf_op jit(solution)/shard_map/all_gather | solution.py:286
  61.4 0.0 collective-permute-done.1.pair_oth
  61.4 0.0 copy-done.1
  61.4 3.5 %tail.1 = f32[2304,128]{1,0:T(8,128)} custom-call(f32[512,256]{1,0:T(8,128)S(1)} %all_gather.3.whole_ref, f32[1,256]{1,0:T(1,128)S(1)} %bitcast.4, f32[2304,128]{1,0:T(8,128)S(1)} %get-tuple-element.17.orb, f32[4608,128]{1,0:T(8,128)S(1)} %get-tuple-element.18.pair, f32[2304,128]{1,0:T(8,128)S(1)} %collective-permute-done.orb_ref.orb_oth, ...), custom_call_target="tpu_custom_call" | custom-call | tf_op jit(solution)/shard_map/tail/pallas_call | solution.py:256
  (2 shorter events, 0.1 us)
Async XLA Ops:
  0.0 13.0 %collective-permute-start = (f32[2304,128]{1,0:T(8,128)}, f32[2304,128]{1,0:T(8,128)S(1)}, u32[]{:S(2)}, u32[]{:S(2)}) collective-permute-start(f32[2304,128]{1,0:T(8,128)} %orb_hbm.1), channel_id=1, source_target_pairs={{0,1},{1,0},{2,3},{3,2},{4,5},{5,4},{6,7},{7,6},{8,9},{9,8},{10,11... | collective-permute-start | bytes 3538952 | tf_op jit(solution)/shard_map/ppermute | solution.py:278
  11.0 11.2 %copy-start = (f32[32,128]{1,0:T(8,128)S(1)}, f32[32,128]{1,0:T(8,128)}, u32[]{:S(2)}) copy-start(f32[32,128]{1,0:T(8,128)} %panel_ref.1) | copy-start | bytes 49156
  11.0 50.4 %collective-permute-start.1 = (f32[4608,128]{1,0:T(8,128)S(1)}, f32[4608,128]{1,0:T(8,128)S(1)}, u32[]{:S(2)}, u32[]{:S(2)}) collective-permute-start(f32[4608,128]{1,0:T(8,128)S(1)} %get-tuple-element.18.pair), channel_id=1, source_target_pairs={{0,1},{1,0},{2,3},{3,2},{4,5},{5,4},{6,7},{7,6},{8,9},{9,8},{10,11... | collective-permute-start | bytes 7077896 | tf_op jit(solution)/shard_map/ppermute | solution.py:281
  22.2 39.2 %copy-start.1 = (f32[256]{0:T(256)S(1)}, f32[256]{0:T(256)}, u32[]{:S(2)}) copy-start(f32[256]{0:T(256)} %param.9) | copy-start | bytes 3076

commit v5 on v4

--- a/solution.py
+++ b/solution.py
@@ -1,3 +1,5 @@
+import itertools
+
 import jax
 import jax.numpy as jnp
 from jax import lax
@@ -14,7 +16,7 @@
 TAIL_CHUNK = 576
 INNER = ((1,), (0,))
 NEAR = ("zn", "x", "yn")
-FAR = ("zf", "yf")
+CELLS = ("zf", "zn", "x", "yf", "yn")
 OCTET = 8
 MIB = 2**20
 
@@ -23,6 +25,31 @@
     return lax.dot_general(
         left, right, (dims, ((), ())), preferred_element_type=F32, precision=precision
     )
+
+
+def mirrored(block, near):
+    return 2 * block + (near + block // 2) % 2
+
+
+def far_groups():
+    return [
+        [
+            mirrored(zf, zn) * 32 + x * 8 + mirrored(yf, yn)
+            for zf, yf in itertools.product(range(4), range(4))
+        ]
+        for zn, x, yn in itertools.product(range(2), range(4), range(2))
+    ]
+
+
+def flips():
+    return lax.axis_index("zf") // 2, lax.axis_index("yf") // 2
+
+
+def place(tile, z_flip, y_flip):
+    zn, x, yn = tile // 8, tile // 2 % 4, tile % 2
+    z = 1 - z_flip if zn else z_flip
+    y = 1 - y_flip if yn else y_flip
+    return 8 * z + 2 * x + y
 
 
 def split(x):
@@ -83,9 +110,14 @@
     for step in range(steps):
         part = dot(cot_t_ref[step], halves(orb_ref[pl.ds(step * chunk, chunk), :], 1))
         total = part if total is None else total + part
-    mine = lax.axis_index("bcol")
-    out_ref[pl.ds(pl.multiple_of(mine * width, width), width), :] = own_ref[...]
-    out_ref[pl.ds(pl.multiple_of((1 - mine) * width, width), width), :] = folded(total)
+    other = folded(total)
+    first = lax.axis_index("bcol") == 0
+    parts = (jnp.where(first, own_ref[...], other), jnp.where(first, other, own_ref[...]))
+    rows = jnp.concatenate(parts, axis=0)
+    turned = flips()
+    tile = out_ref.shape[1]
+    for at in range(out_ref.shape[0]):
+        out_ref[place(at, *turned)] = rows[at * tile : (at + 1) * tile, :]
 
 
 def spread_kernel(parts_ref, panel_ref, out_ref):
@@ -96,7 +128,8 @@
 
 def gather_kernel(parts_ref, out_ref):
     tile = parts_ref.shape[1] - OCTET
-    octets = parts_ref[pl.ds(2 * lax.axis_index("zn"), 2), tile:, :]
+    zn = (lax.axis_index("zn") + flips()[0]) % 2
+    octets = parts_ref[pl.ds(2 * zn, 2), tile:, :]
     total = jnp.sum(parts_ref[:, :tile, :], axis=0)
     both = jnp.concatenate([total, octets.reshape(2 * OCTET, total.shape[1])], axis=0)
     out_ref[...] = jnp.broadcast_to(both[None], out_ref.shape)
@@ -114,15 +147,16 @@
     second = pl.ds(pl.multiple_of((1 - mine) * width, width), width)
     block = 4 * OCTET
     tile = 2 * OCTET
-    sums = jnp.concatenate(
-        [whole_ref[q * block : q * block + tile, :] for q in range(bands // tile)], axis=0
-    )
+    turned = flips()
+    starts = [pl.multiple_of(place(at, *turned) * block, block) for at in range(bands // tile)]
+    sums = jnp.concatenate([whole_ref[pl.ds(start, tile), :] for start in starts], axis=0)
     octets = []
     for y in range(bands // block):
-        yf, yn = y // 2, y % 2
+        zn, slot = y // 4, y // 2 % 2
+        yn = (y + zn) % 2
         for x in range(block // OCTET):
-            at = (8 * (yf // 2) + 2 * x + yn) * block + tile + (yf % 2) * OCTET
-            octets.append(whole_ref[at : at + OCTET, :])
+            start = starts[8 * zn + 2 * x + yn] + (tile + slot * OCTET)
+            octets.append(whole_ref[pl.ds(pl.multiple_of(start, OCTET), OCTET), :])
     half = len(octets) // 2
     top, bottom = (jnp.concatenate(part, axis=0) for part in (octets[:half], octets[half:]))
     grad_t = jnp.concatenate(
@@ -213,11 +247,11 @@
     )(orbitals, applied, cotangent)
 
 
-def whole_gram(own, cot_t, orb_oth):
+def whole_gram(own, cot_t, orb_oth, near):
     cells, width = orb_oth.shape
     return pl.pallas_call(
         other_kernel,
-        out_shape=jax.ShapeDtypeStruct((2 * width, width), F32),
+        out_shape=jax.ShapeDtypeStruct((near, 2 * width // near, width), F32),
         in_specs=[VMEM, VMEM, VMEM],
         out_specs=VMEM,
         compiler_params=limit(10),
@@ -272,16 +306,19 @@
     width = orbitals.shape[1]
     swap = [(0, 1), (1, 0)]
     near = lax.axis_size(NEAR)
-    far = lax.axis_size(FAR)
+    groups = far_groups()
+    far = len(groups[0])
 
     blocks = [pltpu.with_memory_space_constraint(x, pltpu.HBM) for x in (orbitals, applied, cotangent)]
     orb_oth = lax.ppermute(orbitals, "bcol", swap)
     own, cot_t, orb, pair = own_gram(*blocks)
     pair, own, cot_t = lax.optimization_barrier((pair, own, cot_t))
     pair_oth = lax.ppermute(pair, "bcol", swap)
-    partial = whole_gram(own, cot_t, orb_oth)
-    parts = lax.all_to_all(partial.reshape(near, -1, width), NEAR, 0, 0, tiled=True)
-    parts = lax.all_to_all(spread(parts, panel, far), FAR, 0, 0, tiled=True)
+    partial = whole_gram(own, cot_t, orb_oth, near)
+    parts = lax.all_to_all(partial, NEAR, 0, 0, tiled=True)
+    parts = lax.all_to_all(
+        spread(parts, panel, far), CELLS, 0, 0, tiled=True, axis_index_groups=groups
+    )
     sums = lax.all_to_all(gather(parts, near), NEAR, 0, 0, tiled=True)
     whole = lax.all_gather(sums.reshape(-1, width), "bcol", axis=1, tiled=True)
     return tail(whole, levels, orb, pair, orb_oth, pair_oth)
@@ -289,7 +326,7 @@
 
 def solution(mesh):
     fine = Mesh(mesh.devices.reshape(4, 2, 4, 4, 2, 2), ("zf", "zn", "x", "yf", "yn", "bcol"))
-    cells = P(("zf", "zn", "x", "yf", "yn"), "bcol")
+    cells = P(CELLS, "bcol")
     return jax.shard_map(
         body,
         mesh=fine,

time: 65.3 us -> 65.7 us (level)
    all_to_all x1, blocking collectives: 9.28 us -> 12.8 us  [body(): sums = lax.all_to_all(gather(parts, near), NEAR, 0, 0, tiled=True)]
    all_to_all x2, blocking collectives: 32.3 us -> 29.2 us  [the longest x1 20.4 us: body(): lax.all_to_all(spread(parts, panel, far), CELLS, 0, 0, tiled=True, axis_i...]
where the time goes in v5:
time: 65.7 us; the launch traced here: 65.4 us
  blocking collectives  48.3 us (74%)
  starting transfers between devices  10.7 us (16%)
  Pallas kernels  6.35 us (10%)
    all_to_all x1, blocking collectives, body(): lax.all_to_all(spread(parts, panel, far), CELLS, 0, 0, tiled=True, axis_i...  20.4 us
    all_to_all x1, blocking collectives, body(): sums = lax.all_to_all(gather(parts, near), NEAR, 0, 0, tiled=True)  12.8 us
    ppermute x1, starting transfers between devices, body(): orb_oth = lax.ppermute(orbitals, 'bcol', swap)  8.77 us
    all_to_all x1, blocking collectives, body(): parts = lax.all_to_all(partial, NEAR, 0, 0, tiled=True)  8.74 us
    all_gather x1, blocking collectives, body(): whole = lax.all_gather(sums.reshape(-1, width), 'bcol', axis=1, tiled=True)  6.3 us
    pallas_call x1, Pallas kernels, tail(): pl.pallas_call(tail_kernel, out_shape=jax.ShapeDtypeStruct((cells, width)...  3.55 us
    pallas_call x1, Pallas kernels, own_gram(): pl.pallas_call(own_kernel, out_shape=(jax.ShapeDtypeStruct((width, width)...  2.23 us
    ppermute x1, starting transfers between devices, body(): pair_oth = lax.ppermute(pair, 'bcol', swap)  1.92 us
  transfers between devices with their start and end apart: 2, of which 0 were waited for; matrix products, arithmetic and copies ran while one was open for 0% of the time, Pallas kernels for 4%

profile of v5, /device:TPU:1, one launch (start us, length us, event | category | flops | bytes accessed | tf_op | source)
XLA Modules:
  0.0 65.4 jit_solution(17140402203165732076)
XLA Ops:
  0.0 8.8 %collective-permute-start = (f32[2304,128]{1,0:T(8,128)}, f32[2304,128]{1,0:T(8,128)S(1)}, u32[]{:S(2)}, u32[]{:S(2)}) collective-permute-start(f32[2304,128]{1,0:T(8,128)} %orb_hbm.1), channel_id=1, source_target_pairs={{0,1},{1,0},{2,3},{3,2},{4,5},{5,4},{6,7},{7,6},{8,9},{9,8},{10,11... | collective-permute-start | bytes 3538952 | tf_op jit(solution)/shard_map/ppermute | solution.py:313
  8.8 2.2 %own_gram.1 = (f32[128,128]{1,0:T(8,128)S(1)}, bf16[2,256,1152]{2,1,0:T(8,128)(2,1)S(1)}, f32[2304,128]{1,0:T(8,128)S(1)}, f32[4608,128]{1,0:T(8,128)S(1)}) custom-call(f32[2304,128]{1,0:T(8,128)} %orb_hbm.1, f32[2304,128]{1,0:T(8,128)} %app_hbm.1, f32[2304,128]{1,0:T(8,128)} %cot_hbm.1), custom_call_target="tpu_custom_call" | custom-call | flops 301989888 | bytes 3538944 | tf_op jit(solution)/shard_map/own_gram/pallas_call | solution.py:231
  11.0 0.0 copy-start
  11.0 1.9 %collective-permute-start.1 = (f32[4608,128]{1,0:T(8,128)S(1)}, f32[4608,128]{1,0:T(8,128)S(1)}, u32[]{:S(2)}, u32[]{:S(2)}) collective-permute-start(f32[4608,128]{1,0:T(8,128)S(1)} %get-tuple-element.18.pair), channel_id=1, source_target_pairs={{0,1},{1,0},{2,3},{3,2},{4,5},{5,4},{6,7},{7,6},{8,9},{9,8},{10,11... | collective-permute-start | bytes 7077896 | tf_op jit(solution)/shard_map/ppermute | solution.py:316
  13.0 0.0 collective-permute-done.orb_ref.orb_oth
  13.0 0.5 whole_gram.1
  13.5 8.7 %all_to_all.15.parts_ref = f32[16,16,128]{2,1,0:T(8,128)S(1)} all-to-all(f32[16,16,128]{2,1,0:T(8,128)S(1)} %whole_gram.1), channel_id=1, replica_groups=mesh['zf'=4,'zn'=2,'x'=4,'yf'=4,'yn'=2,'bcol'=2] {'zn','x','yn'}, dimensions={0} | all-to-all | bytes 262144 | tf_op jit(solution)/shard_map/all_to_all | solution.py:318
  22.2 0.0 copy-done
  22.2 0.0 copy-start.1
  22.3 20.4 %all_to_all.16.parts_ref = f32[16,24,128]{2,1,0:T(8,128)S(1)} all-to-all(f32[16,24,128]{2,1,0:T(8,128)S(1)} %spread.1), channel_id=1, replica_groups={{0,4,10,14,128,132,138,142,320,324,330,334,448,452,458,462},{2,6,8,12,1..., dimensions={0} | all-to-all | bytes 393216 | tf_op jit(solution)/shard_map/all_to_all | solution.py:319
  42.7 12.8 %all_to_all.17 = f32[16,32,128]{2,1,0:T(8,128)S(1)} all-to-all(f32[16,32,128]{2,1,0:T(8,128)S(1)} %gather.1), channel_id=1, replica_groups=mesh['zf'=4,'zn'=2,'x'=4,'yf'=4,'yn'=2,'bcol'=2] {'zn','x','yn'}, dimensions={0} | all-to-all | bytes 524288 | tf_op jit(solution)/shard_map/all_to_all | solution.py:322
  55.5 6.3 %all_gather.3.whole_ref = f32[512,256]{1,0:T(8,128)S(1)} all-gather(f32[512,128]{1,0:T(8,128)S(1)} %bitcast.3), channel_id=1, replica_groups=mesh['zf'=4,'zn'=2,'x'=4,'yf'=4,'yn'=2,'bcol'=2] {'bcol'}, dimensions={1}, use_global_device_ids=true | all-gather | bytes 786432 | tf_op jit(solution)/shard_map/all_gather | solution.py:323
  61.8 0.0 collective-permute-done.1.pair_oth
  61.8 0.0 copy-done.1
  61.8 3.5 %tail.1 = f32[2304,128]{1,0:T(8,128)} custom-call(f32[512,256]{1,0:T(8,128)S(1)} %all_gather.3.whole_ref, f32[1,256]{1,0:T(1,128)S(1)} %bitcast.2, f32[2304,128]{1,0:T(8,128)S(1)} %get-tuple-element.17.orb, f32[4608,128]{1,0:T(8,128)S(1)} %get-tuple-element.18.pair, f32[2304,128]{1,0:T(8,128)S(1)} %collective-permute-done.orb_ref.orb_oth, ...), custom_call_target="tpu_custom_call" | custom-call | tf_op jit(solution)/shard_map/tail/pallas_call | solution.py:290
  (2 shorter events, 0.1 us)
Async XLA Ops:
  0.0 13.0 %collective-permute-start = (f32[2304,128]{1,0:T(8,128)}, f32[2304,128]{1,0:T(8,128)S(1)}, u32[]{:S(2)}, u32[]{:S(2)}) collective-permute-start(f32[2304,128]{1,0:T(8,128)} %orb_hbm.1), channel_id=1, source_target_pairs={{0,1},{1,0},{2,3},{3,2},{4,5},{5,4},{6,7},{7,6},{8,9},{9,8},{10,11... | collective-permute-start | bytes 3538952 | tf_op jit(solution)/shard_map/ppermute | solution.py:313
  11.0 11.2 %copy-start = (f32[32,128]{1,0:T(8,128)S(1)}, f32[32,128]{1,0:T(8,128)}, u32[]{:S(2)}) copy-start(f32[32,128]{1,0:T(8,128)} %panel_ref.1) | copy-start | bytes 49156
  11.0 50.8 %collective-permute-start.1 = (f32[4608,128]{1,0:T(8,128)S(1)}, f32[4608,128]{1,0:T(8,128)S(1)}, u32[]{:S(2)}, u32[]{:S(2)}) collective-permute-start(f32[4608,128]{1,0:T(8,128)S(1)} %get-tuple-element.18.pair), channel_id=1, source_target_pairs={{0,1},{1,0},{2,3},{3,2},{4,5},{5,4},{6,7},{7,6},{8,9},{9,8},{10,11... | collective-permute-start | bytes 7077896 | tf_op jit(solution)/shard_map/ppermute | solution.py:316
  22.2 39.6 %copy-start.1 = (f32[256]{0:T(256)S(1)}, f32[256]{0:T(256)}, u32[]{:S(2)}) copy-start(f32[256]{0:T(256)} %param.9) | copy-start | bytes 3076

commit v6 on v5

--- a/solution.py
+++ b/solution.py
@@ -27,29 +27,22 @@
     )
 
 
-def mirrored(block, near):
-    return 2 * block + (near + block // 2) % 2
-
-
 def far_groups():
     return [
         [
-            mirrored(zf, zn) * 32 + x * 8 + mirrored(yf, yn)
+            (2 * zf + zn) * 32 + x * 8 + 2 * yf + (yn + yf // 2) % 2
             for zf, yf in itertools.product(range(4), range(4))
         ]
         for zn, x, yn in itertools.product(range(2), range(4), range(2))
     ]
 
 
-def flips():
-    return lax.axis_index("zf") // 2, lax.axis_index("yf") // 2
-
-
-def place(tile, z_flip, y_flip):
-    zn, x, yn = tile // 8, tile // 2 % 4, tile % 2
-    z = 1 - z_flip if zn else z_flip
-    y = 1 - y_flip if yn else y_flip
-    return 8 * z + 2 * x + y
+def upper():
+    return lax.axis_index("yf") // 2
+
+
+def place(tile, mirror):
+    return tile - mirror if tile % 2 else tile + mirror
 
 
 def split(x):
@@ -114,10 +107,10 @@
     first = lax.axis_index("bcol") == 0
     parts = (jnp.where(first, own_ref[...], other), jnp.where(first, other, own_ref[...]))
     rows = jnp.concatenate(parts, axis=0)
-    turned = flips()
+    mirror = upper()
     tile = out_ref.shape[1]
     for at in range(out_ref.shape[0]):
-        out_ref[place(at, *turned)] = rows[at * tile : (at + 1) * tile, :]
+        out_ref[place(at, mirror)] = rows[at * tile : (at + 1) * tile, :]
 
 
 def spread_kernel(parts_ref, panel_ref, out_ref):
@@ -128,8 +121,7 @@
 
 def gather_kernel(parts_ref, out_ref):
     tile = parts_ref.shape[1] - OCTET
-    zn = (lax.axis_index("zn") + flips()[0]) % 2
-    octets = parts_ref[pl.ds(2 * zn, 2), tile:, :]
+    octets = parts_ref[pl.ds(2 * lax.axis_index("zn"), 2), tile:, :]
     total = jnp.sum(parts_ref[:, :tile, :], axis=0)
     both = jnp.concatenate([total, octets.reshape(2 * OCTET, total.shape[1])], axis=0)
     out_ref[...] = jnp.broadcast_to(both[None], out_ref.shape)
@@ -147,8 +139,8 @@
     second = pl.ds(pl.multiple_of((1 - mine) * width, width), width)
     block = 4 * OCTET
     tile = 2 * OCTET
-    turned = flips()
-    starts = [pl.multiple_of(place(at, *turned) * block, block) for at in range(bands // tile)]
+    mirror = upper()
+    starts = [pl.multiple_of(place(at, mirror) * block, block) for at in range(bands // tile)]
     sums = jnp.concatenate([whole_ref[pl.ds(start, tile), :] for start in starts], axis=0)
     octets = []
     for y in range(bands // block):

time: 65.7 us -> 64.8 us (0.986)
  blocking collectives: 48.3 us -> 47.3 us
    all_to_all x1, blocking collectives: 12.8 us -> 10.3 us  [body(): sums = lax.all_to_all(gather(parts, near), NEAR, 0, 0, tiled=True)]
    all_to_all x1, blocking collectives: 20.4 us -> 22.5 us  [body(): lax.all_to_all(spread(parts, panel, far), CELLS, 0, 0, tiled=True, axis_i...]
where the time goes in v6:
time: 64.8 us; the launch traced here: 64.4 us
  blocking collectives  47.3 us (73%)
  starting transfers between devices  10.7 us (17%)
  Pallas kernels  6.33 us (10%)
    all_to_all x1, blocking collectives, body(): lax.all_to_all(spread(parts, panel, far), CELLS, 0, 0, tiled=True, axis_i...  22.5 us
    all_to_all x1, blocking collectives, body(): sums = lax.all_to_all(gather(parts, near), NEAR, 0, 0, tiled=True)  10.3 us
    ppermute x1, starting transfers between devices, body(): orb_oth = lax.ppermute(orbitals, 'bcol', swap)  8.77 us
    all_to_all x1, blocking collectives, body(): parts = lax.all_to_all(partial, NEAR, 0, 0, tiled=True)  8.74 us
    all_gather x1, blocking collectives, body(): whole = lax.all_gather(sums.reshape(-1, width), 'bcol', axis=1, tiled=True)  5.77 us
    pallas_call x1, Pallas kernels, tail(): pl.pallas_call(tail_kernel, out_shape=jax.ShapeDtypeStruct((cells, width)...  3.53 us
    pallas_call x1, Pallas kernels, own_gram(): pl.pallas_call(own_kernel, out_shape=(jax.ShapeDtypeStruct((width, width)...  2.23 us
    ppermute x1, starting transfers between devices, body(): pair_oth = lax.ppermute(pair, 'bcol', swap)  1.92 us
  transfers between devices with their start and end apart: 2, of which 0 were waited for; matrix products, arithmetic and copies ran while one was open for 0% of the time, Pallas kernels for 4%

profile of v6, /device:TPU:1, one launch (start us, length us, event | category | flops | bytes accessed | tf_op | source)
XLA Modules:
  0.0 64.4 jit_solution(1740343235813119495)
XLA Ops:
  0.0 8.8 %collective-permute-start = (f32[2304,128]{1,0:T(8,128)}, f32[2304,128]{1,0:T(8,128)S(1)}, u32[]{:S(2)}, u32[]{:S(2)}) collective-permute-start(f32[2304,128]{1,0:T(8,128)} %orb_hbm.1), channel_id=1, source_target_pairs={{0,1},{1,0},{2,3},{3,2},{4,5},{5,4},{6,7},{7,6},{8,9},{9,8},{10,11... | collective-permute-start | bytes 3538952 | tf_op jit(solution)/shard_map/ppermute | solution.py:305
  8.8 2.2 %own_gram.1 = (f32[128,128]{1,0:T(8,128)S(1)}, bf16[2,256,1152]{2,1,0:T(8,128)(2,1)S(1)}, f32[2304,128]{1,0:T(8,128)S(1)}, f32[4608,128]{1,0:T(8,128)S(1)}) custom-call(f32[2304,128]{1,0:T(8,128)} %orb_hbm.1, f32[2304,128]{1,0:T(8,128)} %app_hbm.1, f32[2304,128]{1,0:T(8,128)} %cot_hbm.1), custom_call_target="tpu_custom_call" | custom-call | flops 301989888 | bytes 3538944 | tf_op jit(solution)/shard_map/own_gram/pallas_call | solution.py:223
  11.0 0.0 copy-start
  11.0 1.9 %collective-permute-start.1 = (f32[4608,128]{1,0:T(8,128)S(1)}, f32[4608,128]{1,0:T(8,128)S(1)}, u32[]{:S(2)}, u32[]{:S(2)}) collective-permute-start(f32[4608,128]{1,0:T(8,128)S(1)} %get-tuple-element.18.pair), channel_id=1, source_target_pairs={{0,1},{1,0},{2,3},{3,2},{4,5},{5,4},{6,7},{7,6},{8,9},{9,8},{10,11... | collective-permute-start | bytes 7077896 | tf_op jit(solution)/shard_map/ppermute | solution.py:308
  13.0 0.0 collective-permute-done.orb_ref.orb_oth
  13.0 0.5 whole_gram.1
  13.5 8.7 %all_to_all.15.parts_ref = f32[16,16,128]{2,1,0:T(8,128)S(1)} all-to-all(f32[16,16,128]{2,1,0:T(8,128)S(1)} %whole_gram.1), channel_id=1, replica_groups=mesh['zf'=4,'zn'=2,'x'=4,'yf'=4,'yn'=2,'bcol'=2] {'zn','x','yn'}, dimensions={0} | all-to-all | bytes 262144 | tf_op jit(solution)/shard_map/all_to_all | solution.py:310
  22.2 0.0 copy-done
  22.2 0.0 copy-start.1
  22.3 22.5 %all_to_all.16.parts_ref = f32[16,24,128]{2,1,0:T(8,128)S(1)} all-to-all(f32[16,24,128]{2,1,0:T(8,128)S(1)} %spread.1), channel_id=1, replica_groups={{0,4,10,14,128,132,138,142,256,260,266,270,384,388,394,398},{2,6,8,12,1..., dimensions={0} | all-to-all | bytes 393216 | tf_op jit(solution)/shard_map/all_to_all | solution.py:311
  44.8 10.3 %all_to_all.17 = f32[16,32,128]{2,1,0:T(8,128)S(1)} all-to-all(f32[16,32,128]{2,1,0:T(8,128)S(1)} %gather.1), channel_id=1, replica_groups=mesh['zf'=4,'zn'=2,'x'=4,'yf'=4,'yn'=2,'bcol'=2] {'zn','x','yn'}, dimensions={0} | all-to-all | bytes 524288 | tf_op jit(solution)/shard_map/all_to_all | solution.py:314
  55.1 5.8 %all_gather.3.whole_ref = f32[512,256]{1,0:T(8,128)S(1)} all-gather(f32[512,128]{1,0:T(8,128)S(1)} %bitcast.3), channel_id=1, replica_groups=mesh['zf'=4,'zn'=2,'x'=4,'yf'=4,'yn'=2,'bcol'=2] {'bcol'}, dimensions={1}, use_global_device_ids=true | all-gather | bytes 786432 | tf_op jit(solution)/shard_map/all_gather | solution.py:315
  60.9 0.0 collective-permute-done.1.pair_oth
  60.9 0.0 copy-done.1
  60.9 3.5 %tail.1 = f32[2304,128]{1,0:T(8,128)} custom-call(f32[512,256]{1,0:T(8,128)S(1)} %all_gather.3.whole_ref, f32[1,256]{1,0:T(1,128)S(1)} %bitcast.2, f32[2304,128]{1,0:T(8,128)S(1)} %get-tuple-element.17.orb, f32[4608,128]{1,0:T(8,128)S(1)} %get-tuple-element.18.pair, f32[2304,128]{1,0:T(8,128)S(1)} %collective-permute-done.orb_ref.orb_oth, ...), custom_call_target="tpu_custom_call" | custom-call | tf_op jit(solution)/shard_map/tail/pallas_call | solution.py:282
  (2 shorter events, 0.1 us)
Async XLA Ops:
  0.0 13.0 %collective-permute-start = (f32[2304,128]{1,0:T(8,128)}, f32[2304,128]{1,0:T(8,128)S(1)}, u32[]{:S(2)}, u32[]{:S(2)}) collective-permute-start(f32[2304,128]{1,0:T(8,128)} %orb_hbm.1), channel_id=1, source_target_pairs={{0,1},{1,0},{2,3},{3,2},{4,5},{5,4},{6,7},{7,6},{8,9},{9,8},{10,11... | collective-permute-start | bytes 3538952 | tf_op jit(solution)/shard_map/ppermute | solution.py:305
  11.0 11.2 %copy-start = (f32[32,128]{1,0:T(8,128)S(1)}, f32[32,128]{1,0:T(8,128)}, u32[]{:S(2)}) copy-start(f32[32,128]{1,0:T(8,128)} %panel_ref.1) | copy-start | bytes 49156
  11.0 49.9 %collective-permute-start.1 = (f32[4608,128]{1,0:T(8,128)S(1)}, f32[4608,128]{1,0:T(8,128)S(1)}, u32[]{:S(2)}, u32[]{:S(2)}) collective-permute-start(f32[4608,128]{1,0:T(8,128)S(1)} %get-tuple-element.18.pair), channel_id=1, source_target_pairs={{0,1},{1,0},{2,3},{3,2},{4,5},{5,4},{6,7},{7,6},{8,9},{9,8},{10,11... | collective-permute-start | bytes 7077896 | tf_op jit(solution)/shard_map/ppermute | solution.py:308
  22.2 38.7 %copy-start.1 = (f32[256]{0:T(256)S(1)}, f32[256]{0:T(256)}, u32[]{:S(2)}) copy-start(f32[256]{0:T(256)} %param.9) | copy-start | bytes 3076

commit v7 on v6

--- a/solution.py
+++ b/solution.py
@@ -17,6 +17,7 @@
 INNER = ((1,), (0,))
 NEAR = ("zn", "x", "yn")
 CELLS = ("zf", "zn", "x", "yf", "yn")
+QUARTET = 4
 OCTET = 8
 MIB = 2**20
 
@@ -114,17 +115,25 @@
 
 
 def spread_kernel(parts_ref, panel_ref, out_ref):
-    octet = pl.ds(pl.multiple_of(lax.axis_index("x") * OCTET, OCTET), OCTET)
-    both = jnp.concatenate([jnp.sum(parts_ref[...], axis=0), panel_ref[octet, :]], axis=0)
-    out_ref[...] = jnp.broadcast_to(both[None], out_ref.shape)
-
-
-def gather_kernel(parts_ref, out_ref):
-    tile = parts_ref.shape[1] - OCTET
-    octets = parts_ref[pl.ds(2 * lax.axis_index("zn"), 2), tile:, :]
-    total = jnp.sum(parts_ref[:, :tile, :], axis=0)
-    both = jnp.concatenate([total, octets.reshape(2 * OCTET, total.shape[1])], axis=0)
-    out_ref[...] = jnp.broadcast_to(both[None], out_ref.shape)
+    total = jnp.sum(parts_ref[...], axis=0)
+    shape = (out_ref.shape[0],) + out_ref.shape[2:]
+    last = out_ref.shape[1] - 1
+    for at in range(last):
+        out_ref[:, at] = jnp.broadcast_to(total[at * QUARTET : (at + 1) * QUARTET, :][None], shape)
+    x = lax.axis_index("x")
+    octet = panel_ref[pl.ds(pl.multiple_of((2 * lax.axis_index("zn") + x // 2) * OCTET, OCTET), OCTET), :]
+    quartet = jnp.where(x % 2 == 0, octet[:QUARTET, :], octet[QUARTET:, :])
+    out_ref[:, last] = jnp.broadcast_to(quartet[None], shape)
+
+
+def gather_kernel(parts_ref, out_ref, block):
+    last = parts_ref.shape[1] - 1
+    for at in range(last):
+        block[at * QUARTET : (at + 1) * QUARTET, :] = jnp.sum(parts_ref[:, at], axis=0)
+    for yf in range(4):
+        start = (last + yf) * QUARTET
+        block[start : start + QUARTET, :] = parts_ref[yf, last]
+    out_ref[...] = jnp.broadcast_to(block[...][None], out_ref.shape)
 
 
 def tail_kernel(
@@ -143,12 +152,21 @@
     starts = [pl.multiple_of(place(at, mirror) * block, block) for at in range(bands // tile)]
     sums = jnp.concatenate([whole_ref[pl.ds(start, tile), :] for start in starts], axis=0)
     octets = []
+    above = lax.broadcasted_iota(jnp.int32, (OCTET, bands), 0) < QUARTET
     for y in range(bands // block):
-        zn, slot = y // 4, y // 2 % 2
-        yn = (y + zn) % 2
-        for x in range(block // OCTET):
-            start = starts[8 * zn + 2 * x + yn] + (tile + slot * OCTET)
-            octets.append(whole_ref[pl.ds(pl.multiple_of(start, OCTET), OCTET), :])
+        yf = y // 2
+        yn = (y + yf // 2) % 2
+        for octet in range(block // OCTET):
+            near = 8 * (octet // 2) + 4 * (octet % 2) + yn
+            first_quartet, second_quartet = (
+                whole_ref[pl.ds(pl.multiple_of(starts[at] + (tile + yf // 2 * OCTET), OCTET), OCTET), :]
+                for at in (near, near + 2)
+            )
+            if yf % 2:
+                first_quartet = pltpu.roll(first_quartet, QUARTET, 0)
+            else:
+                second_quartet = pltpu.roll(second_quartet, QUARTET, 0)
+            octets.append(jnp.where(above, first_quartet, second_quartet))
     half = len(octets) // 2
     top, bottom = (jnp.concatenate(part, axis=0) for part in (octets[:half], octets[half:]))
     grad_t = jnp.concatenate(
@@ -247,6 +265,7 @@
         in_specs=[VMEM, VMEM, VMEM],
         out_specs=VMEM,
         compiler_params=limit(10),
+        cost_estimate=pl.CostEstimate(flops=8 * cells * width * width, bytes_accessed=8 * cells * width, transcendentals=0),
         name="whole_gram",
     )(own, cot_t, orb_oth)
 
@@ -255,7 +274,7 @@
     near, tile, width = parts.shape
     return pl.pallas_call(
         spread_kernel,
-        out_shape=jax.ShapeDtypeStruct((receivers, tile + OCTET, width), F32),
+        out_shape=jax.ShapeDtypeStruct((receivers, tile // QUARTET + 1, QUARTET, width), F32),
         in_specs=[VMEM, VMEM],
         out_specs=VMEM,
         compiler_params=limit(2),
@@ -264,12 +283,14 @@
 
 
 def gather(parts, receivers):
-    far, rows, width = parts.shape
+    far, quartets, rows, width = parts.shape
+    height = (quartets - 1 + 4) * rows
     return pl.pallas_call(
         gather_kernel,
-        out_shape=jax.ShapeDtypeStruct((receivers, rows + OCTET, width), F32),
+        out_shape=jax.ShapeDtypeStruct((receivers, height, width), F32),
         in_specs=[VMEM],
         out_specs=VMEM,
+        scratch_shapes=[pltpu.VMEM((height, width), F32)],
         compiler_params=limit(2),
         name="gather",
     )(parts)

time: 64.8 us -> 64.9 us (level)
  no operation moved by 1% of the time
where the time goes in v7:
time: 64.9 us; the launch traced here: 64.5 us
  blocking collectives  47.4 us (73%)
  starting transfers between devices  10.7 us (16%)
  Pallas kernels  6.37 us (10%)
    all_to_all x1, blocking collectives, body(): lax.all_to_all(spread(parts, panel, far), CELLS, 0, 0, tiled=True, axis_i...  22.3 us
    all_to_all x1, blocking collectives, body(): sums = lax.all_to_all(gather(parts, near), NEAR, 0, 0, tiled=True)  10.3 us
    ppermute x1, starting transfers between devices, body(): orb_oth = lax.ppermute(orbitals, 'bcol', swap)  8.77 us
    all_to_all x1, blocking collectives, body(): parts = lax.all_to_all(partial, NEAR, 0, 0, tiled=True)  8.74 us
    all_gather x1, blocking collectives, body(): whole = lax.all_gather(sums.reshape(-1, width), 'bcol', axis=1, tiled=True)  6.05 us
    pallas_call x1, Pallas kernels, tail(): pl.pallas_call(tail_kernel, out_shape=jax.ShapeDtypeStruct((cells, width)...  3.55 us
    pallas_call x1, Pallas kernels, own_gram(): pl.pallas_call(own_kernel, out_shape=(jax.ShapeDtypeStruct((width, width)...  2.23 us
    ppermute x1, starting transfers between devices, body(): pair_oth = lax.ppermute(pair, 'bcol', swap)  1.92 us
  transfers between devices with their start and end apart: 2, of which 0 were waited for; matrix products, arithmetic and copies ran while one was open for 0% of the time, Pallas kernels for 4%

profile of v7, /device:TPU:1, one launch (start us, length us, event | category | flops | bytes accessed | tf_op | source)
XLA Modules:
  0.0 64.5 jit_solution(2679695522864715804)
XLA Ops:
  0.0 8.8 %collective-permute-start = (f32[2304,128]{1,0:T(8,128)}, f32[2304,128]{1,0:T(8,128)S(1)}, u32[]{:S(2)}, u32[]{:S(2)}) collective-permute-start(f32[2304,128]{1,0:T(8,128)} %orb_hbm.1), channel_id=1, source_target_pairs={{0,1},{1,0},{2,3},{3,2},{4,5},{5,4},{6,7},{7,6},{8,9},{9,8},{10,11... | collective-permute-start | bytes 3538952 | tf_op jit(solution)/shard_map/ppermute | solution.py:326
  8.8 2.2 %own_gram.1 = (f32[128,128]{1,0:T(8,128)S(1)}, bf16[2,256,1152]{2,1,0:T(8,128)(2,1)S(1)}, f32[2304,128]{1,0:T(8,128)S(1)}, f32[4608,128]{1,0:T(8,128)S(1)}) custom-call(f32[2304,128]{1,0:T(8,128)} %orb_hbm.1, f32[2304,128]{1,0:T(8,128)} %app_hbm.1, f32[2304,128]{1,0:T(8,128)} %cot_hbm.1), custom_call_target="tpu_custom_call" | custom-call | flops 301989888 | bytes 3538944 | tf_op jit(solution)/shard_map/own_gram/pallas_call | solution.py:241
  11.0 0.0 copy-start
  11.0 1.9 %collective-permute-start.1 = (f32[4608,128]{1,0:T(8,128)S(1)}, f32[4608,128]{1,0:T(8,128)S(1)}, u32[]{:S(2)}, u32[]{:S(2)}) collective-permute-start(f32[4608,128]{1,0:T(8,128)S(1)} %get-tuple-element.18.pair), channel_id=1, source_target_pairs={{0,1},{1,0},{2,3},{3,2},{4,5},{5,4},{6,7},{7,6},{8,9},{9,8},{10,11... | collective-permute-start | bytes 7077896 | tf_op jit(solution)/shard_map/ppermute | solution.py:329
  13.0 0.0 collective-permute-done.orb_ref.orb_oth
  13.0 0.5 whole_gram.1
  13.5 8.7 %all_to_all.15.parts_ref = f32[16,16,128]{2,1,0:T(8,128)S(1)} all-to-all(f32[16,16,128]{2,1,0:T(8,128)S(1)} %whole_gram.1), channel_id=1, replica_groups=mesh['zf'=4,'zn'=2,'x'=4,'yf'=4,'yn'=2,'bcol'=2] {'zn','x','yn'}, dimensions={0} | all-to-all | bytes 262144 | tf_op jit(solution)/shard_map/all_to_all | solution.py:331
  22.2 0.0 copy-done
  22.2 0.0 copy-start.1
  22.3 22.3 %all_to_all.16.parts_ref = f32[16,5,4,128]{3,2,1,0:T(4,128)S(1)} all-to-all(f32[16,5,4,128]{3,2,1,0:T(4,128)S(1)} %spread.1), channel_id=1, replica_groups={{0,4,10,14,128,132,138,142,256,260,266,270,384,388,394,398},{2,6,8,12,1..., dimensions={0} | all-to-all | bytes 327680 | tf_op jit(solution)/shard_map/all_to_all | solution.py:332
  44.6 10.3 %all_to_all.17 = f32[16,32,128]{2,1,0:T(8,128)S(1)} all-to-all(f32[16,32,128]{2,1,0:T(8,128)S(1)} %gather.1), channel_id=1, replica_groups=mesh['zf'=4,'zn'=2,'x'=4,'yf'=4,'yn'=2,'bcol'=2] {'zn','x','yn'}, dimensions={0} | all-to-all | bytes 524288 | tf_op jit(solution)/shard_map/all_to_all | solution.py:335
  54.9 6.0 %all_gather.3.whole_ref = f32[512,256]{1,0:T(8,128)S(1)} all-gather(f32[512,128]{1,0:T(8,128)S(1)} %bitcast.3), channel_id=1, replica_groups=mesh['zf'=4,'zn'=2,'x'=4,'yf'=4,'yn'=2,'bcol'=2] {'bcol'}, dimensions={1}, use_global_device_ids=true | all-gather | bytes 786432 | tf_op jit(solution)/shard_map/all_gather | solution.py:336
  61.0 0.0 collective-permute-done.1.pair_oth
  61.0 0.0 copy-done.1
  61.0 3.5 %tail.1 = f32[2304,128]{1,0:T(8,128)} custom-call(f32[512,256]{1,0:T(8,128)S(1)} %all_gather.3.whole_ref, f32[1,256]{1,0:T(1,128)S(1)} %bitcast.2, f32[2304,128]{1,0:T(8,128)S(1)} %get-tuple-element.17.orb, f32[4608,128]{1,0:T(8,128)S(1)} %get-tuple-element.18.pair, f32[2304,128]{1,0:T(8,128)S(1)} %collective-permute-done.orb_ref.orb_oth, ...), custom_call_target="tpu_custom_call" | custom-call | tf_op jit(solution)/shard_map/tail/pallas_call | solution.py:303
  (2 shorter events, 0.1 us)
Async XLA Ops:
  0.0 13.0 %collective-permute-start = (f32[2304,128]{1,0:T(8,128)}, f32[2304,128]{1,0:T(8,128)S(1)}, u32[]{:S(2)}, u32[]{:S(2)}) collective-permute-start(f32[2304,128]{1,0:T(8,128)} %orb_hbm.1), channel_id=1, source_target_pairs={{0,1},{1,0},{2,3},{3,2},{4,5},{5,4},{6,7},{7,6},{8,9},{9,8},{10,11... | collective-permute-start | bytes 3538952 | tf_op jit(solution)/shard_map/ppermute | solution.py:326
  11.0 11.2 %copy-start = (f32[32,128]{1,0:T(8,128)S(1)}, f32[32,128]{1,0:T(8,128)}, u32[]{:S(2)}) copy-start(f32[32,128]{1,0:T(8,128)} %panel_ref.1) | copy-start | bytes 49156
  11.0 50.0 %collective-permute-start.1 = (f32[4608,128]{1,0:T(8,128)S(1)}, f32[4608,128]{1,0:T(8,128)S(1)}, u32[]{:S(2)}, u32[]{:S(2)}) collective-permute-start(f32[4608,128]{1,0:T(8,128)S(1)} %get-tuple-element.18.pair), channel_id=1, source_target_pairs={{0,1},{1,0},{2,3},{3,2},{4,5},{5,4},{6,7},{7,6},{8,9},{9,8},{10,11... | collective-permute-start | bytes 7077896 | tf_op jit(solution)/shard_map/ppermute | solution.py:329
  22.2 38.8 %copy-start.1 = (f32[256]{0:T(256)S(1)}, f32[256]{0:T(256)}, u32[]{:S(2)}) copy-start(f32[256]{0:T(256)} %param.9) | copy-start | bytes 3076

commit v8 on v6

--- a/solution.py
+++ b/solution.py
@@ -31,7 +31,7 @@
     return [
         [
             (2 * zf + zn) * 32 + x * 8 + 2 * yf + (yn + yf // 2) % 2
-            for zf, yf in itertools.product(range(4), range(4))
+            for zf, yf in itertools.product((2, 1, 3, 0), range(4))
         ]
         for zn, x, yn in itertools.product(range(2), range(4), range(2))
     ]

time: 64.8 us -> 62.8 us (0.969)
  blocking collectives: 47.3 us -> 45.3 us
    all_to_all x1, blocking collectives: 22.5 us -> 21.3 us  [body(): lax.all_to_all(spread(parts, panel, far), CELLS, 0, 0, tiled=True, axis_i...]
    all_to_all x1, blocking collectives: 10.3 us -> 9.39 us  [body(): sums = lax.all_to_all(gather(parts, near), NEAR, 0, 0, tiled=True)]
where the time goes in v8:
time: 62.8 us; the launch traced here: 62.5 us
  blocking collectives  45.3 us (72%)
  starting transfers between devices  10.7 us (17%)
  Pallas kernels  6.34 us (10%)
    all_to_all x1, blocking collectives, body(): lax.all_to_all(spread(parts, panel, far), CELLS, 0, 0, tiled=True, axis_i...  21.3 us
    all_to_all x1, blocking collectives, body(): sums = lax.all_to_all(gather(parts, near), NEAR, 0, 0, tiled=True)  9.39 us
    ppermute x1, starting transfers between devices, body(): orb_oth = lax.ppermute(orbitals, 'bcol', swap)  8.77 us
    all_to_all x1, blocking collectives, body(): parts = lax.all_to_all(partial, NEAR, 0, 0, tiled=True)  8.74 us
    all_gather x1, blocking collectives, body(): whole = lax.all_gather(sums.reshape(-1, width), 'bcol', axis=1, tiled=True)  5.96 us
    pallas_call x1, Pallas kernels, tail(): pl.pallas_call(tail_kernel, out_shape=jax.ShapeDtypeStruct((cells, width)...  3.54 us
    pallas_call x1, Pallas kernels, own_gram(): pl.pallas_call(own_kernel, out_shape=(jax.ShapeDtypeStruct((width, width)...  2.23 us
    ppermute x1, starting transfers between devices, body(): pair_oth = lax.ppermute(pair, 'bcol', swap)  1.92 us
  transfers between devices with their start and end apart: 2, of which 0 were waited for; matrix products, arithmetic and copies ran while one was open for 0% of the time, Pallas kernels for 4%

profile of v8, /device:TPU:1, one launch (start us, length us, event | category | flops | bytes accessed | tf_op | source)
XLA Modules:
  0.0 62.5 jit_solution(6548398508092903417)
XLA Ops:
  0.0 8.8 %collective-permute-start = (f32[2304,128]{1,0:T(8,128)}, f32[2304,128]{1,0:T(8,128)S(1)}, u32[]{:S(2)}, u32[]{:S(2)}) collective-permute-start(f32[2304,128]{1,0:T(8,128)} %orb_hbm.1), channel_id=1, source_target_pairs={{0,1},{1,0},{2,3},{3,2},{4,5},{5,4},{6,7},{7,6},{8,9},{9,8},{10,11... | collective-permute-start | bytes 3538952 | tf_op jit(solution)/shard_map/ppermute | solution.py:305
  8.8 2.2 %own_gram.1 = (f32[128,128]{1,0:T(8,128)S(1)}, bf16[2,256,1152]{2,1,0:T(8,128)(2,1)S(1)}, f32[2304,128]{1,0:T(8,128)S(1)}, f32[4608,128]{1,0:T(8,128)S(1)}) custom-call(f32[2304,128]{1,0:T(8,128)} %orb_hbm.1, f32[2304,128]{1,0:T(8,128)} %app_hbm.1, f32[2304,128]{1,0:T(8,128)} %cot_hbm.1), custom_call_target="tpu_custom_call" | custom-call | flops 301989888 | bytes 3538944 | tf_op jit(solution)/shard_map/own_gram/pallas_call | solution.py:223
  11.0 0.0 copy-start
  11.0 1.9 %collective-permute-start.1 = (f32[4608,128]{1,0:T(8,128)S(1)}, f32[4608,128]{1,0:T(8,128)S(1)}, u32[]{:S(2)}, u32[]{:S(2)}) collective-permute-start(f32[4608,128]{1,0:T(8,128)S(1)} %get-tuple-element.18.pair), channel_id=1, source_target_pairs={{0,1},{1,0},{2,3},{3,2},{4,5},{5,4},{6,7},{7,6},{8,9},{9,8},{10,11... | collective-permute-start | bytes 7077896 | tf_op jit(solution)/shard_map/ppermute | solution.py:308
  13.0 0.0 collective-permute-done.orb_ref.orb_oth
  13.0 0.5 whole_gram.1
  13.5 8.7 %all_to_all.15.parts_ref = f32[16,16,128]{2,1,0:T(8,128)S(1)} all-to-all(f32[16,16,128]{2,1,0:T(8,128)S(1)} %whole_gram.1), channel_id=1, replica_groups=mesh['zf'=4,'zn'=2,'x'=4,'yf'=4,'yn'=2,'bcol'=2] {'zn','x','yn'}, dimensions={0} | all-to-all | bytes 262144 | tf_op jit(solution)/shard_map/all_to_all | solution.py:310
  22.2 0.0 copy-done
  22.2 0.0 copy-start.1
  22.3 21.3 %all_to_all.16.parts_ref = f32[16,24,128]{2,1,0:T(8,128)S(1)} all-to-all(f32[16,24,128]{2,1,0:T(8,128)S(1)} %spread.1), channel_id=1, replica_groups={{256,260,266,270,128,132,138,142,384,388,394,398,0,4,10,14},{258,262,26..., dimensions={0} | all-to-all | bytes 393216 | tf_op jit(solution)/shard_map/all_to_all | solution.py:311
  43.6 9.4 %all_to_all.17 = f32[16,32,128]{2,1,0:T(8,128)S(1)} all-to-all(f32[16,32,128]{2,1,0:T(8,128)S(1)} %gather.1), channel_id=1, replica_groups=mesh['zf'=4,'zn'=2,'x'=4,'yf'=4,'yn'=2,'bcol'=2] {'zn','x','yn'}, dimensions={0} | all-to-all | bytes 524288 | tf_op jit(solution)/shard_map/all_to_all | solution.py:314
  52.9 6.0 %all_gather.3.whole_ref = f32[512,256]{1,0:T(8,128)S(1)} all-gather(f32[512,128]{1,0:T(8,128)S(1)} %bitcast.3), channel_id=1, replica_groups=mesh['zf'=4,'zn'=2,'x'=4,'yf'=4,'yn'=2,'bcol'=2] {'bcol'}, dimensions={1}, use_global_device_ids=true | all-gather | bytes 786432 | tf_op jit(solution)/shard_map/all_gather | solution.py:315
  58.9 0.0 collective-permute-done.1.pair_oth
  58.9 0.0 copy-done.1
  58.9 3.5 %tail.1 = f32[2304,128]{1,0:T(8,128)} custom-call(f32[512,256]{1,0:T(8,128)S(1)} %all_gather.3.whole_ref, f32[1,256]{1,0:T(1,128)S(1)} %bitcast.2, f32[2304,128]{1,0:T(8,128)S(1)} %get-tuple-element.17.orb, f32[4608,128]{1,0:T(8,128)S(1)} %get-tuple-element.18.pair, f32[2304,128]{1,0:T(8,128)S(1)} %collective-permute-done.orb_ref.orb_oth, ...), custom_call_target="tpu_custom_call" | custom-call | tf_op jit(solution)/shard_map/tail/pallas_call | solution.py:282
  (2 shorter events, 0.1 us)
Async XLA Ops:
  0.0 13.0 %collective-permute-start = (f32[2304,128]{1,0:T(8,128)}, f32[2304,128]{1,0:T(8,128)S(1)}, u32[]{:S(2)}, u32[]{:S(2)}) collective-permute-start(f32[2304,128]{1,0:T(8,128)} %orb_hbm.1), channel_id=1, source_target_pairs={{0,1},{1,0},{2,3},{3,2},{4,5},{5,4},{6,7},{7,6},{8,9},{9,8},{10,11... | collective-permute-start | bytes 3538952 | tf_op jit(solution)/shard_map/ppermute | solution.py:305
  11.0 11.2 %copy-start = (f32[32,128]{1,0:T(8,128)S(1)}, f32[32,128]{1,0:T(8,128)}, u32[]{:S(2)}) copy-start(f32[32,128]{1,0:T(8,128)} %panel_ref.1) | copy-start | bytes 49156
  11.0 47.9 %collective-permute-start.1 = (f32[4608,128]{1,0:T(8,128)S(1)}, f32[4608,128]{1,0:T(8,128)S(1)}, u32[]{:S(2)}, u32[]{:S(2)}) collective-permute-start(f32[4608,128]{1,0:T(8,128)S(1)} %get-tuple-element.18.pair), channel_id=1, source_target_pairs={{0,1},{1,0},{2,3},{3,2},{4,5},{5,4},{6,7},{7,6},{8,9},{9,8},{10,11... | collective-permute-start | bytes 7077896 | tf_op jit(solution)/shard_map/ppermute | solution.py:308
  22.2 36.7 %copy-start.1 = (f32[256]{0:T(256)S(1)}, f32[256]{0:T(256)}, u32[]{:S(2)}) copy-start(f32[256]{0:T(256)} %param.9) | copy-start | bytes 3076

commit v9 on v8

--- a/solution.py
+++ b/solution.py
@@ -31,7 +31,7 @@
     return [
         [
             (2 * zf + zn) * 32 + x * 8 + 2 * yf + (yn + yf // 2) % 2
-            for zf, yf in itertools.product((2, 1, 3, 0), range(4))
+            for zf, yf in itertools.product((2, 1, 3, 0), (2, 1, 3, 0))
         ]
         for zn, x, yn in itertools.product(range(2), range(4), range(2))
     ]
@@ -121,7 +121,8 @@
 
 def gather_kernel(parts_ref, out_ref):
     tile = parts_ref.shape[1] - OCTET
-    octets = parts_ref[pl.ds(2 * lax.axis_index("zn"), 2), tile:, :]
+    zn = lax.axis_index("zn")
+    octets = jnp.stack([parts_ref[3 - 3 * zn, tile:, :], parts_ref[1 + zn, tile:, :]])
     total = jnp.sum(parts_ref[:, :tile, :], axis=0)
     both = jnp.concatenate([total, octets.reshape(2 * OCTET, total.shape[1])], axis=0)
     out_ref[...] = jnp.broadcast_to(both[None], out_ref.shape)

time: 62.8 us -> 59.7 us (0.951)
  blocking collectives: 45.3 us -> 42.2 us
    all_to_all x1, blocking collectives: 21.3 us -> 18.4 us  [body(): lax.all_to_all(spread(parts, panel, far), CELLS, 0, 0, tiled=True, axis_i...]
  transfers between devices with their start and end apart: 2 -> 2, of which waited for: 0 -> 0; matrix products, arithmetic and copies ran while one was open for 0% -> 0% of each run, Pallas kernels for 4% -> 5%
where the time goes in v9:
time: 59.7 us; the launch traced here: 59.3 us
  blocking collectives  42.2 us (71%)
  starting transfers between devices  10.7 us (18%)
  Pallas kernels  6.33 us (11%)
    all_to_all x1, blocking collectives, body(): lax.all_to_all(spread(parts, panel, far), CELLS, 0, 0, tiled=True, axis_i...  18.4 us
    all_to_all x1, blocking collectives, body(): sums = lax.all_to_all(gather(parts, near), NEAR, 0, 0, tiled=True)  9.24 us
    ppermute x1, starting transfers between devices, body(): orb_oth = lax.ppermute(orbitals, 'bcol', swap)  8.77 us
    all_to_all x1, blocking collectives, body(): parts = lax.all_to_all(partial, NEAR, 0, 0, tiled=True)  8.74 us
    all_gather x1, blocking collectives, body(): whole = lax.all_gather(sums.reshape(-1, width), 'bcol', axis=1, tiled=True)  5.88 us
    pallas_call x1, Pallas kernels, tail(): pl.pallas_call(tail_kernel, out_shape=jax.ShapeDtypeStruct((cells, width)...  3.53 us
    pallas_call x1, Pallas kernels, own_gram(): pl.pallas_call(own_kernel, out_shape=(jax.ShapeDtypeStruct((width, width)...  2.23 us
    ppermute x1, starting transfers between devices, body(): pair_oth = lax.ppermute(pair, 'bcol', swap)  1.92 us
  transfers between devices with their start and end apart: 2, of which 0 were waited for; matrix products, arithmetic and copies ran while one was open for 0% of the time, Pallas kernels for 5%

profile of v9, /device:TPU:1, one launch (start us, length us, event | category | flops | bytes accessed | tf_op | source)
XLA Modules:
  0.0 59.3 jit_solution(6685896568680413855)
XLA Ops:
  0.0 8.8 %collective-permute-start = (f32[2304,128]{1,0:T(8,128)}, f32[2304,128]{1,0:T(8,128)S(1)}, u32[]{:S(2)}, u32[]{:S(2)}) collective-permute-start(f32[2304,128]{1,0:T(8,128)} %orb_hbm.1), channel_id=1, source_target_pairs={{0,1},{1,0},{2,3},{3,2},{4,5},{5,4},{6,7},{7,6},{8,9},{9,8},{10,11... | collective-permute-start | bytes 3538952 | tf_op jit(solution)/shard_map/ppermute | solution.py:306
  8.8 2.2 %own_gram.1 = (f32[128,128]{1,0:T(8,128)S(1)}, bf16[2,256,1152]{2,1,0:T(8,128)(2,1)S(1)}, f32[2304,128]{1,0:T(8,128)S(1)}, f32[4608,128]{1,0:T(8,128)S(1)}) custom-call(f32[2304,128]{1,0:T(8,128)} %orb_hbm.1, f32[2304,128]{1,0:T(8,128)} %app_hbm.1, f32[2304,128]{1,0:T(8,128)} %cot_hbm.1), custom_call_target="tpu_custom_call" | custom-call | flops 301989888 | bytes 3538944 | tf_op jit(solution)/shard_map/own_gram/pallas_call | solution.py:224
  11.0 0.0 copy-start
  11.0 1.9 %collective-permute-start.1 = (f32[4608,128]{1,0:T(8,128)S(1)}, f32[4608,128]{1,0:T(8,128)S(1)}, u32[]{:S(2)}, u32[]{:S(2)}) collective-permute-start(f32[4608,128]{1,0:T(8,128)S(1)} %get-tuple-element.18.pair), channel_id=1, source_target_pairs={{0,1},{1,0},{2,3},{3,2},{4,5},{5,4},{6,7},{7,6},{8,9},{9,8},{10,11... | collective-permute-start | bytes 7077896 | tf_op jit(solution)/shard_map/ppermute | solution.py:309
  13.0 0.0 collective-permute-done.orb_ref.orb_oth
  13.0 0.5 whole_gram.1
  13.5 8.7 %all_to_all.15.parts_ref = f32[16,16,128]{2,1,0:T(8,128)S(1)} all-to-all(f32[16,16,128]{2,1,0:T(8,128)S(1)} %whole_gram.1), channel_id=1, replica_groups=mesh['zf'=4,'zn'=2,'x'=4,'yf'=4,'yn'=2,'bcol'=2] {'zn','x','yn'}, dimensions={0} | all-to-all | bytes 262144 | tf_op jit(solution)/shard_map/all_to_all | solution.py:311
  22.2 0.0 copy-done
  22.2 0.0 copy-start.1
  22.3 18.4 %all_to_all.16.parts_ref = f32[16,24,128]{2,1,0:T(8,128)S(1)} all-to-all(f32[16,24,128]{2,1,0:T(8,128)S(1)} %spread.1), channel_id=1, replica_groups={{266,260,270,256,138,132,142,128,394,388,398,384,10,4,14,0},{264,262,26..., dimensions={0} | all-to-all | bytes 393216 | tf_op jit(solution)/shard_map/all_to_all | solution.py:312
  40.7 9.2 %all_to_all.17 = f32[16,32,128]{2,1,0:T(8,128)S(1)} all-to-all(f32[16,32,128]{2,1,0:T(8,128)S(1)} %gather.1), channel_id=1, replica_groups=mesh['zf'=4,'zn'=2,'x'=4,'yf'=4,'yn'=2,'bcol'=2] {'zn','x','yn'}, dimensions={0} | all-to-all | bytes 524288 | tf_op jit(solution)/shard_map/all_to_all | solution.py:315
  49.9 5.9 %all_gather.3.whole_ref = f32[512,256]{1,0:T(8,128)S(1)} all-gather(f32[512,128]{1,0:T(8,128)S(1)} %bitcast.3), channel_id=1, replica_groups=mesh['zf'=4,'zn'=2,'x'=4,'yf'=4,'yn'=2,'bcol'=2] {'bcol'}, dimensions={1}, use_global_device_ids=true | all-gather | bytes 786432 | tf_op jit(solution)/shard_map/all_gather | solution.py:316
  55.8 0.0 collective-permute-done.1.pair_oth
  55.8 0.0 copy-done.1
  55.8 3.5 %tail.1 = f32[2304,128]{1,0:T(8,128)} custom-call(f32[512,256]{1,0:T(8,128)S(1)} %all_gather.3.whole_ref, f32[1,256]{1,0:T(1,128)S(1)} %bitcast.2, f32[2304,128]{1,0:T(8,128)S(1)} %get-tuple-element.17.orb, f32[4608,128]{1,0:T(8,128)S(1)} %get-tuple-element.18.pair, f32[2304,128]{1,0:T(8,128)S(1)} %collective-permute-done.orb_ref.orb_oth, ...), custom_call_target="tpu_custom_call" | custom-call | tf_op jit(solution)/shard_map/tail/pallas_call | solution.py:283
  (2 shorter events, 0.1 us)
Async XLA Ops:
  0.0 13.0 %collective-permute-start = (f32[2304,128]{1,0:T(8,128)}, f32[2304,128]{1,0:T(8,128)S(1)}, u32[]{:S(2)}, u32[]{:S(2)}) collective-permute-start(f32[2304,128]{1,0:T(8,128)} %orb_hbm.1), channel_id=1, source_target_pairs={{0,1},{1,0},{2,3},{3,2},{4,5},{5,4},{6,7},{7,6},{8,9},{9,8},{10,11... | collective-permute-start | bytes 3538952 | tf_op jit(solution)/shard_map/ppermute | solution.py:306
  11.0 11.2 %copy-start = (f32[32,128]{1,0:T(8,128)S(1)}, f32[32,128]{1,0:T(8,128)}, u32[]{:S(2)}) copy-start(f32[32,128]{1,0:T(8,128)} %panel_ref.1) | copy-start | bytes 49156
  11.0 44.8 %collective-permute-start.1 = (f32[4608,128]{1,0:T(8,128)S(1)}, f32[4608,128]{1,0:T(8,128)S(1)}, u32[]{:S(2)}, u32[]{:S(2)}) collective-permute-start(f32[4608,128]{1,0:T(8,128)S(1)} %get-tuple-element.18.pair), channel_id=1, source_target_pairs={{0,1},{1,0},{2,3},{3,2},{4,5},{5,4},{6,7},{7,6},{8,9},{9,8},{10,11... | collective-permute-start | bytes 7077896 | tf_op jit(solution)/shard_map/ppermute | solution.py:309
  22.2 33.6 %copy-start.1 = (f32[256]{0:T(256)S(1)}, f32[256]{0:T(256)}, u32[]{:S(2)}) copy-start(f32[256]{0:T(256)} %param.9) | copy-start | bytes 3076
